TPU v7x, 32 devices: a whole 2x2x4 slice. The times are simulated.
32 devices in a mesh: dp: 8 (over y, x, core), rep: 4 (over z).
Axes of the slice: x: 2, y: 2, z: 4, core: 2. Of those that a mesh axis runs over, the one named last changes fastest.
Arguments:
- inputs: bfloat16 [2, 4, 2048, 1024], P(None, 'rep', 'dp'), may hold values from -6 to 6
- skips: bfloat16 [2, 4, 2048, 1024], P(None, 'rep', 'dp'), may hold values from -6 to 6
- cotangent: bfloat16 [2, 4, 2048, 1024], P(None, 'rep', 'dp'), may hold values from -6 to 6
- dest_slot: int32 [2, 4, 256], P(None, 'rep', 'dp'), may hold values from 0 to 255, as said below
- pack_segments: int32 [2, 4, 2048], P(None, 'rep', 'dp'), may hold values from 0 to 15, as said below
- block_live: int32 [2, 4, 256], P(None, 'rep', 'dp'), may hold values from 4 to 8
- counts: int32 [8, 4], P('dp', 'rep'), may hold values from 64 to 208
- w_skip: bfloat16 [2048, 1024], P('rep'), may hold values from -0.125 to 0.125
- b_skip: float32 [1024], replicated, may hold values from -3 to 3
- g_one: float32 [1024], replicated, may hold values from 0.1 to 1.9
- b_one: float32 [1024], replicated, may hold values from -3 to 3
- w_qkv: bfloat16 [1024, 3072], P('rep'), may hold values from -0.25 to 0.25
- w_out: bfloat16 [1024, 1024], P('rep'), may hold values from -0.75 to 0.75
- b_out: float32 [1024], replicated, may hold values from -3 to 3
- g_two: float32 [1024], replicated, may hold values from 0.1 to 1.9
- b_two: float32 [1024], replicated, may hold values from -3 to 3
- w_up: bfloat16 [1024, 4096], P('rep'), may hold values from -0.1875 to 0.1875
- c_up: float32 [4096], replicated, may hold values from -3 to 3
- w_down: bfloat16 [4096, 1024], P('rep'), may hold values from -0.09375 to 0.09375
- c_down: float32 [1024], replicated, may hold values from -3 to 3
Outputs:
- output: bfloat16 [2, 4, 2048, 1024], P(None, 'rep', 'dp')
- input_grad: bfloat16 [2, 4, 2048, 1024], P(None, 'rep', 'dp')
- skip_grad: bfloat16 [2, 4, 2048, 1024], P(None, 'rep', 'dp')
- grad_w_skip: float32 [2048, 1024], P('dp')
- grad_b_skip: float32 [1024], replicated
- grad_g_one: float32 [1024], replicated
- grad_b_one: float32 [1024], replicated
- grad_w_qkv: float32 [1024, 3072], P('dp')
- grad_w_out: float32 [1024, 1024], P('dp')
- grad_b_out: float32 [1024], replicated
- grad_g_two: float32 [1024], replicated
- grad_b_two: float32 [1024], replicated
- grad_w_up: float32 [1024, 4096], P('dp')
- grad_c_up: float32 [4096], replicated
- grad_w_down: float32 [4096, 1024], P('dp')
- grad_c_down: float32 [1024], replicated
Inputs may be any that keep to these rules, and one draw needn't show every extreme that they name: `dest_slot`: for each micro-batch and replica, each slot is named by exactly one block; of one device's 32 blocks, the same number name slots of each device's range d * 32 to d * 32 + 31. `pack_segments`: within the 256 frames of one pack, ids never fall and start at 0; in every draw some pack holds a single utterance, and some pack reaches the largest id.
All inputs are finite; a program needn't handle non-finite values.
Results may differ from a plain program's by a relative error of at most 0.02.
Values may be sent and summed in bfloat16 or wider, within the bound.
No kernel may reach another device: no remote copies, remote signals or barrier semaphores. Data moves between devices by JAX's collectives and lax.ppermute only.
A program may use at most 256 MiB of HBM per device.

v0:
```python
import jax
import jax.numpy as jnp
from jax import lax
from jax.experimental import pallas as pl
from jax.experimental.pallas import tpu as pltpu
from jax.sharding import PartitionSpec as P

HEADS = 16
HEAD = 64
EPS = 1e-05
F32 = jnp.float32
BF16 = jnp.bfloat16
TOKEN = jax.ShapeDtypeStruct((8, 128), F32)
ANY = pl.BlockSpec(memory_space=pl.ANY)
LIGHT = pl.CostEstimate(flops=1024, bytes_accessed=1024, transcendentals=0)


def flip(value, bit):
    n = lax.axis_size("dp")
    return lax.ppermute(value, "dp", [(i, i ^ bit) for i in range(n)])


def rep_flip(value, bit):
    n = lax.axis_size("rep")
    return lax.ppermute(value, "rep", [(i, i ^ bit) for i in range(n)])


def after(value, *earlier):
    return lax.optimization_barrier((value,) + earlier)[0]


def together(*values):
    return lax.optimization_barrier(values)


def assemble(w_local, parts, place, row_at, tiles, deps=()):
    rep = lax.axis_size("rep")
    shard_rows, columns = w_local.shape
    rows = shard_rows // 8
    tile = columns // tiles
    half = tile // 2
    chunk_rows = parts[0][0].shape[0] // (len(parts[0][1]) * (rep - 1))
    arrays = [part[0] for part in parts]
    count = 1 + sum(len(part[1]) for part in parts) * (rep - 1) * tiles

    def body(place_ref, local_ref, *refs):
        out_ref, token_ref, sems = refs[-3:]
        token_ref[...] = jnp.zeros_like(token_ref)
        z = place_ref[0]
        e = place_ref[1]
        copies = [
            pltpu.make_async_copy(
                local_ref,
                out_ref.at[pl.ds(pl.multiple_of(z * shard_rows, 16), shard_rows), :],
                sems.at[0],
            )
        ]
        for ref, (_, runs) in zip(refs, parts):
            for k, (side, rel) in enumerate(runs):
                chunk = jnp.bitwise_xor(e, rel)
                for s, apart in enumerate(far_order(rep), 1):
                    shard = jnp.bitwise_xor(z, apart)
                    start = pl.multiple_of(shard * shard_rows + chunk * rows, 16)
                    for t in range(tiles):
                        at = (k * (rep - 1) + s - 1) * chunk_rows + row_at + t * rows
                        copies.append(
                            pltpu.make_async_copy(
                                ref.at[pl.ds(at, rows), :],
                                out_ref.at[pl.ds(start, rows), pl.ds(t * tile + side * half, half)],
                                sems.at[len(copies)],
                            )
                        )
        for copy in copies:
            copy.start()
        for copy in copies:
            copy.wait()

    return pl.pallas_call(
        body,
        out_shape=[jax.ShapeDtypeStruct((shard_rows * rep, columns), w_local.dtype), TOKEN],
        grid=(1,),
        in_specs=[pl.BlockSpec(memory_space=pltpu.SMEM)] + [ANY] * (1 + len(parts) + len(deps)),
        out_specs=[
            pl.BlockSpec((shard_rows * rep, columns), lambda i: (0, 0)),
            pl.BlockSpec(TOKEN.shape, lambda i: (0, 0)),
        ],
        scratch_shapes=[pltpu.SemaphoreType.DMA((count,))],
        compiler_params=pltpu.CompilerParams(vmem_limit_bytes=26 * 2**20),
        cost_estimate=pl.CostEstimate(flops=int(1.5 * 1.15e9), bytes_accessed=1024, transcendentals=0),
        name="assemble",
    )(place, w_local, *arrays, *deps)


def own_chunk(place, width, shards_local, deps=()):
    items = []
    for which, w_local in enumerate(shards_local):
        for t in range(w_local.shape[1] // width):
            items.append((which, w_local.shape[0] // 8, t * width))
    total = sum(item[1] for item in items)

    def body(place_ref, *refs):
        out_ref, sems = refs[-2:]
        copies = []
        at = 0
        for which, rows, column in items:
            start = pl.multiple_of(place_ref[1] * rows, 16)
            copies.append(
                pltpu.make_async_copy(
                    refs[which].at[pl.ds(start, rows), pl.ds(column, width)],
                    out_ref.at[pl.ds(at, rows), :],
                    sems.at[len(copies)],
                )
            )
            at += rows
        for copy in copies:
            copy.start()
        for copy in copies:
            copy.wait()

    return pl.pallas_call(
        body,
        out_shape=jax.ShapeDtypeStruct((total, width), shards_local[0].dtype),
        grid=(1,),
        in_specs=[pl.BlockSpec(memory_space=pltpu.SMEM)]
        + [ANY] * (len(shards_local) + len(deps)),
        out_specs=pl.BlockSpec((total, width), lambda i: (0, 0)),
        scratch_shapes=[pltpu.SemaphoreType.DMA((len(items),))],
        compiler_params=pltpu.CompilerParams(vmem_limit_bytes=24 * 2**20),
        cost_estimate=LIGHT,
        name="own_chunk",
    )(place, *shards_local, *deps)


def pack(arrays, outs, deps=()):
    count = sum(len(out) for out in outs)

    def body(*refs):
        sources, targets = refs[: len(arrays)], refs[-2 - len(outs) : -2]
        token_ref, sems = refs[-2:]
        token_ref[...] = jnp.zeros_like(token_ref)
        copies = []
        for target, out in zip(targets, outs):
            at = 0
            for which, row, rows, column, columns in out:
                copies.append(
                    pltpu.make_async_copy(
                        sources[which].at[pl.ds(row, rows), pl.ds(column, columns)],
                        target.at[pl.ds(at, rows), :],
                        sems.at[len(copies)],
                    )
                )
                at += rows
        for copy in copies:
            copy.start()
        for copy in copies:
            copy.wait()

    return pl.pallas_call(
        body,
        out_shape=[
            jax.ShapeDtypeStruct((sum(item[2] for item in out), out[0][4]), arrays[0].dtype)
            for out in outs
        ]
        + [TOKEN],
        grid=(1,),
        in_specs=[ANY] * (len(arrays) + len(deps)),
        out_specs=[
            pl.BlockSpec((sum(item[2] for item in out), out[0][4]), lambda i: (0, 0))
            for out in outs
        ]
        + [pl.BlockSpec(TOKEN.shape, lambda i: (0, 0))],
        scratch_shapes=[pltpu.SemaphoreType.DMA((count,))],
        compiler_params=pltpu.CompilerParams(vmem_limit_bytes=24 * 2**20),
        cost_estimate=LIGHT,
        name="pack",
    )(*arrays, *deps)


def far_order(rep):
    order = [0]
    for bit in reversed(range(rep.bit_length() - 1)):
        order = order + [distance ^ (1 << bit) for distance in order]
    return order[1:]


class Spread:
    def __init__(self, gots, width, deps=()):
        self.half = width // 2
        rows = sum(got.shape[0] for got in gots)
        items = [(i, 0, got.shape[0]) for i, got in enumerate(gots)]
        *self.start, _ = pack(
            gots, [[item + (column, self.half) for item in items] for column in (0, self.half)], deps
        )
        self.n = rows

    def near(self):
        return [flip(self.start[0], 2), flip(self.start[1], 4)]

    def near_landed(self, got, deps=()):
        whole = [(i, 0, self.n, 0, self.half) for i in range(4)]
        *self.pairs, self.token = pack(
            [self.start[0], got[0], self.start[1], got[1]], [whole[:2], whole[2:]], deps
        )

    def cross(self):
        return [flip(self.pairs[0], 4), flip(self.pairs[1], 2)]

    def cross_landed(self, got, deps=()):
        whole = [(i, 0, 2 * self.n, 0, self.half) for i in range(4)]
        self.every, self.token = pack([self.pairs[0], got[0], self.pairs[1], got[1]], [whole], deps)

    def share(self):
        return flip(self.every, 1)

    def parts(self, other):
        runs = [(0, 0), (0, 2), (0, 4), (0, 6), (1, 0), (1, 4), (1, 2), (1, 6)]
        return [(self.every, runs), (other, [(side, rel | 1) for side, rel in runs])]


def rep_steps(rep):
    return [1 << bit for bit in reversed(range(rep.bit_length() - 1))]


class Fetch:
    def __init__(self, own):
        self.held = [own]
        self.steps = rep_steps(lax.axis_size("rep"))

    def send(self, deps=()):
        sent = self.held[0]
        if len(self.held) > 1:
            whole = [(i, 0, a.shape[0], 0, a.shape[1]) for i, a in enumerate(self.held)]
            sent, _ = pack(self.held, [whole], deps)
        return rep_flip(sent, self.steps[len(self.held) - 1])

    def landed(self, got):
        self.held.append(got)

    def rest(self):
        while len(self.held) < len(self.steps):
            self.landed(self.send())

    def far(self):
        return self.held[1:]


def plan_order(all_slots, all_live, codes, d, block, deps=()):
    micro, owners = all_slots.shape
    frames = codes.shape[1]
    blocks = frames // block
    dp = owners // blocks
    per_pair = blocks // dp
    total = micro * frames

    def column(row):
        return jnp.broadcast_to(row, (128, row.shape[1])).T[:, :1]

    def as_row(values):
        return jnp.broadcast_to(values, (values.shape[0], 128)).T[:1, :]

    def body(d_ref, slots_ref, live_ref, codes_ref, *refs):
        far_ref, turned_ref, keep_ref, shuffle_ref = refs[-4:]
        me = d_ref[0]
        lane = lax.broadcasted_iota(jnp.int32, (1, owners), 1)
        source = jnp.bitwise_xor(lax.div(lane, jnp.int32(blocks)), me)
        first_slot = (source * blocks).astype(F32) + lax.rem(lane, jnp.int32(blocks)).astype(F32)
        source_col = column(source.astype(F32))
        frame = lax.broadcasted_iota(jnp.int32, (frames, 1), 0)
        block_of = lax.div(frame, jnp.int32(block)).astype(F32)
        inner = lax.rem(frame, jnp.int32(block)).astype(F32)
        low = (me * blocks).astype(F32)
        rows = []
        for m in range(micro):
            slots = slots_ref[pl.ds(m, 1), :]
            slots_col = column(slots)
            same = source_col == source.astype(F32)
            rank = jnp.sum(jnp.where(same & (slots_col < slots), 1.0, 0.0), axis=0, keepdims=True)
            here = (slots >= low) & (slots < low + blocks)
            arrive = source.astype(F32) * per_pair + rank - (me * per_pair).astype(F32)
            arrive = jnp.where(here, arrive, -1.0)
            placed = jnp.sum(
                jnp.where(arrive == block_of, slots - low, 0.0), axis=1, keepdims=True
            )
            position = placed * block + inner
            at = lax.broadcasted_iota(jnp.int32, (1, frames), 1).astype(F32)
            code = jnp.sum(
                jnp.where(at == position, codes_ref[pl.ds(m, 1), :], 0.0), axis=1, keepdims=True
            )
            position_row, code_row = as_row(position), as_row(code)
            segment, segment_row = jnp.floor(code * 0.5), jnp.floor(code_row * 0.5)
            live_row = code_row - 2.0 * segment_row
            distance = jnp.abs(position - position_row)
            allowed = (segment == segment_row) & ((live_row > 0.5) | (distance < 0.5))
            far_ref[m] = jnp.where(allowed, distance, 1e32)
            live_col = code - 2.0 * segment
            allowed = (segment == segment_row) & ((live_col > 0.5) | (distance < 0.5))
            turned_ref[m] = jnp.where(allowed, distance, 1e32)
            own = lane < blocks
            mine = jnp.sum(
                jnp.where(own & (lane.astype(F32) == block_of), slots, 0.0), axis=1, keepdims=True
            )
            alive = jnp.sum(
                jnp.where(first_slot == mine, live_ref[pl.ds(m, 1), :], 0.0), axis=1, keepdims=True
            )
            keep_ref[pl.ds(m * frames, frames), :] = jnp.broadcast_to(
                jnp.where(inner < alive, 1.0, 0.0), (frames, 128)
            )
            my_rank = jnp.sum(
                jnp.where(own & (lane.astype(F32) == block_of), rank, 0.0), axis=1, keepdims=True
            )
            target = jnp.floor((my_rank + 0.5) / per_pair)
            row = (target * micro + m) * per_pair + (my_rank - target * per_pair)
            rows.append(as_row(row * block + inner))
        goal = jnp.concatenate(rows, axis=1)
        spot = lax.broadcasted_iota(jnp.int32, (total, total), 0).astype(F32)
        shuffle_ref[...] = jnp.where(spot == goal, 1.0, 0.0).astype(BF16)

    vmem = pl.BlockSpec(memory_space=pltpu.VMEM)
    return pl.pallas_call(
        body,
        out_shape=[
            jax.ShapeDtypeStruct((micro, frames, frames), F32),
            jax.ShapeDtypeStruct((micro, frames, frames), F32),
            jax.ShapeDtypeStruct((total, 128), F32),
            jax.ShapeDtypeStruct((total, total), BF16),
        ],
        in_specs=[pl.BlockSpec(memory_space=pltpu.SMEM), vmem, vmem, vmem] + [ANY] * len(deps),
        out_specs=[vmem, vmem, vmem, vmem],
        compiler_params=pltpu.CompilerParams(vmem_limit_bytes=24 * 2**20),
        cost_estimate=LIGHT,
        name="plan_order",
    )(d.reshape(1).astype(jnp.int32), all_slots, all_live, codes, *deps)


def gradient_blocks(pairs, d, dims, got=None, deps=()):
    dp = lax.axis_size("dp")
    total, all_rows = pairs[0][0].shape
    widths = [right.shape[2] for _, right in pairs]
    columns = sum(right.shape[0] * right.shape[2] for _, right in pairs)
    rows = all_rows // dp
    count = dp // 2
    odd = 1 if got is None else 0
    tile = min(min(widths), 512)
    splits = [width // tile for width in widths]
    tiles = [right.shape[0] * split for (_, right), split in zip(pairs, splits)]
    steps = sum(tiles)
    starts = [sum(tiles[:i]) for i in range(len(tiles))]

    def distance(p):
        rel = odd
        for k, bit in enumerate(dims):
            rel += ((p >> (len(dims) - 1 - k)) & 1) << bit
        return rel

    upper = [p for p in range(count) if p >= count // 2]
    lower = [p for p in range(count) if p < count // 2]
    odds = [p for p in range(count) if p % 2 == 1]
    evens = [p for p in range(count) if p % 2 == 0]
    chosen = (upper, lower, odds, evens)

    if rows % 128 != 0:
        products = []
        for left, right in pairs:
            flat = jnp.transpose(right, (1, 0, 2)).reshape(total, -1)
            products.append(matmul_tn(left, flat))
        product = jnp.concatenate(products, axis=1).reshape(dp, rows, columns)
        rel = jnp.array([distance(p) for p in range(count)], jnp.int32)
        product = product[jnp.bitwise_xor(rel, d)]
        token = jnp.zeros(TOKEN.shape, F32) + product[0, :1, :1]
        if got is None:
            return [product.astype(BF16), token]
        product = (product + jnp.concatenate(got, axis=2).astype(F32)).astype(BF16)
        half = columns // 2
        return [
            jnp.stack([product[p, :, side * half : (side + 1) * half] for p in ps])
            for side, ps in zip((0, 0, 1, 1), chosen)
        ] + [token]

    def body(d_ref, *refs):
        lefts = refs[: len(pairs)]
        rights = refs[len(pairs) : 2 * len(pairs)]
        got_refs = refs[2 * len(pairs) : 3 * len(pairs)]
        token_ref, turned_ref = refs[-2:]
        outs = refs[-3:-2] if got is None else refs[-6:-2]
        c = pl.program_id(0)

        @pl.when(c == 0)
        def _():
            token_ref[...] = jnp.zeros_like(token_ref)
            for i, left_ref in enumerate(lefts):
                for p in range(count):
                    at = pl.multiple_of(jnp.bitwise_xor(d_ref[0], distance(p)) * rows, 128)
                    turned_ref[i, pl.ds(p * rows, rows), :] = left_ref[:, pl.ds(at, rows)].T

        def piece(i, p):
            return jnp.dot(
                turned_ref[i, pl.ds(p * rows, rows), :], rights[i][0], preferred_element_type=F32
            )

        def write(i, half):
            for p in range(count):
                value = piece(i, p)
                if got is None:
                    outs[0][p] = value.astype(BF16)
                    continue
                value = (value + got_refs[i][p].astype(F32)).astype(BF16)
                for which in (2 * half, 2 * half + 1):
                    if p in chosen[which]:
                        outs[which][chosen[which].index(p)] = value

        for i in range(len(pairs)):
            for half in (0, 1):
                low = max(starts[i], half * (steps // 2))
                high = min(starts[i] + tiles[i], (half + 1) * (steps // 2))
                if low < high:
                    pl.when((c >= low) & (c < high))(lambda i=i, half=half: write(i, half))

    def right_spec(start, n, split):
        def at(c, d_ref):
            k = jnp.clip(c - start, 0, n - 1)
            return (lax.div(k, jnp.int32(split)), 0, lax.rem(k, jnp.int32(split)))

        return pl.BlockSpec((1, total, tile), at)

    in_specs = [pl.BlockSpec((total, all_rows), lambda c, d_ref: (0, 0))] * len(pairs)
    in_specs += [right_spec(*item) for item in zip(starts, tiles, splits)]
    args = [left for left, _ in pairs] + [right for _, right in pairs]
    if got is None:
        out_shape = [jax.ShapeDtypeStruct((count, rows, columns), BF16)]
        out_specs = [pl.BlockSpec((count, rows, tile), lambda c, d_ref: (0, 0, c))]
    else:
        for start, n in zip(starts, tiles):
            in_specs.append(
                pl.BlockSpec(
                    (count, rows, tile),
                    lambda c, d_ref, start=start, n=n: (0, 0, jnp.clip(c - start, 0, n - 1)),
                )
            )
        args += got
        out_shape = [jax.ShapeDtypeStruct((count // 2, rows, columns // 2), BF16)] * 4
        mid = steps // 2
        first = pl.BlockSpec(
            (count // 2, rows, tile), lambda c, d_ref: (0, 0, jnp.minimum(c, mid - 1))
        )
        second = pl.BlockSpec(
            (count // 2, rows, tile), lambda c, d_ref: (0, 0, jnp.maximum(c - mid, 0))
        )
        out_specs = [first, first, second, second]
    out_shape = out_shape + [TOKEN]
    out_specs = out_specs + [pl.BlockSpec(TOKEN.shape, lambda c, d_ref: (0, 0))]
    in_specs += [ANY] * len(deps)
    return pl.pallas_call(
        body,
        out_shape=out_shape,
        grid_spec=pltpu.PrefetchScalarGridSpec(
            num_scalar_prefetch=1,
            grid=(steps,),
            in_specs=in_specs,
            out_specs=out_specs,
            scratch_shapes=[pltpu.VMEM((len(pairs), count * rows, total), BF16)],
        ),
        compiler_params=pltpu.CompilerParams(vmem_limit_bytes=34 * 2**20),
        cost_estimate=pl.CostEstimate(flops=int(2.5 * 1.15e9), bytes_accessed=1024, transcendentals=0),
        name="gradient",
    )(d.reshape(1).astype(jnp.int32), *args, *deps)


def head_probs(q, k, far, slope):
    scores = lax.dot_general(q, k, (((1,), (1,)), ((), ())), preferred_element_type=F32)
    scores = scores * (HEAD ** (-0.5)) - slope * far
    raised = jnp.exp(scores - jnp.max(scores, axis=-1, keepdims=True))
    return raised * (1.0 / jnp.sum(raised, axis=-1, keepdims=True))


def flat_frames(block):
    sources, _, rows, lanes = block.shape
    if rows % 16 == 0:
        return block.reshape(sources * rows, lanes)
    return block.astype(F32).reshape(sources * rows, lanes).astype(BF16)


def by_source(value, like):
    sources, _, rows, lanes = like
    if rows % 16 == 0:
        return value.astype(BF16).reshape(sources, 1, rows, lanes)
    return value.reshape(sources, 1, rows, lanes).astype(BF16)


def attend(triple, far, slopes, deps=()):
    dp, micro, rows, wide = triple.shape
    frames = dp * rows
    width = wide // 3
    pairs = width // 128
    shape = (dp, 1, rows, 128)

    def body(slope_ref, q_ref, k_ref, v_ref, far_ref, *refs):
        out_ref = refs[-1]
        h = pl.program_id(1)
        q, k, v = (flat_frames(ref[...]) for ref in (q_ref, k_ref, v_ref))
        first = lax.broadcasted_iota(jnp.int32, (frames, 128), 1) < HEAD
        zero = jnp.zeros_like(q)
        outs = []
        for j, own in enumerate((jnp.where(first, q, zero), jnp.where(first, zero, q))):
            probs = head_probs(own, k, far_ref[0], slope_ref[h * 2 + j])
            outs.append(jnp.dot(probs.astype(BF16), v, preferred_element_type=F32))
        out_ref[...] = by_source(jnp.where(first, outs[0], outs[1]), shape)

    def spec(offset):
        return pl.BlockSpec(shape, lambda m, h, s: (0, m, 0, h + offset))

    return pl.pallas_call(
        body,
        out_shape=jax.ShapeDtypeStruct((dp, micro, rows, width), BF16),
        grid_spec=pltpu.PrefetchScalarGridSpec(
            num_scalar_prefetch=1,
            grid=(micro, pairs),
            in_specs=[
                spec(0),
                spec(pairs),
                spec(2 * pairs),
                pl.BlockSpec((1, frames, frames), lambda m, h, s: (m, 0, 0)),
            ]
            + [ANY] * len(deps),
            out_specs=spec(0),
        ),
        compiler_params=pltpu.CompilerParams(vmem_limit_bytes=24 * 2**20),
        cost_estimate=pl.CostEstimate(flops=int(8 * 1.15e9), bytes_accessed=1024, transcendentals=0),
        name="attend",
    )(slopes, triple, triple, triple, far, *deps)


def attend_back(triple, grad, far, slopes, deps=()):
    dp, micro, rows, wide = triple.shape
    frames = dp * rows
    width = wide // 3
    pairs = width // 128
    shape = (dp, 1, rows, 128)
    scale = HEAD ** (-0.5)

    def turned(left, right):
        return lax.dot_general(left, right, (((0,), (0,)), ((), ())), preferred_element_type=F32)

    def body(slope_ref, q_ref, k_ref, v_ref, g_ref, far_ref, *refs):
        out_ref, token_ref = refs[-2:]
        token_ref[...] = jnp.zeros_like(token_ref)
        h = pl.program_id(1)
        q, k, v, g = (flat_frames(ref[...]) for ref in (q_ref, k_ref, v_ref, g_ref))
        first = lax.broadcasted_iota(jnp.int32, (frames, 128), 1) < HEAD
        zero = jnp.zeros_like(q)
        grads = []
        for j in range(2):
            own_q = jnp.where(first, q, zero) if j == 0 else jnp.where(first, zero, q)
            own_g = jnp.where(first, g, zero) if j == 0 else jnp.where(first, zero, g)
            scores = nt(k, own_q) * scale - slope_ref[h * 2 + j] * far_ref[0]
            raised = jnp.exp(scores - jnp.max(scores, axis=0, keepdims=True))
            probs = raised * (1.0 / jnp.sum(raised, axis=0, keepdims=True))
            back = nt(v, own_g)
            back = probs * (back - jnp.sum(back * probs, axis=0, keepdims=True))
            low = back.astype(BF16)
            grads.append(
                (
                    turned(low, k) * scale,
                    jnp.dot(low, q, preferred_element_type=F32) * scale,
                    jnp.dot(probs.astype(BF16), g, preferred_element_type=F32),
                )
            )
        for i in range(3):
            out_ref[i] = by_source(jnp.where(first, grads[0][i], grads[1][i]), shape)

    def spec(offset):
        return pl.BlockSpec(shape, lambda m, h, s: (0, m, 0, h + offset))

    return pl.pallas_call(
        body,
        out_shape=[jax.ShapeDtypeStruct((3, dp, micro, rows, width), BF16), TOKEN],
        grid_spec=pltpu.PrefetchScalarGridSpec(
            num_scalar_prefetch=1,
            grid=(micro, pairs),
            in_specs=[
                spec(0),
                spec(pairs),
                spec(2 * pairs),
                spec(0),
                pl.BlockSpec((1, frames, frames), lambda m, h, s: (m, 0, 0)),
            ]
            + [ANY] * len(deps),
            out_specs=[
                pl.BlockSpec((3,) + shape, lambda m, h, s: (0, 0, m, 0, h)),
                pl.BlockSpec(TOKEN.shape, lambda m, h, s: (0, 0)),
            ],
        ),
        compiler_params=pltpu.CompilerParams(vmem_limit_bytes=24 * 2**20),
        cost_estimate=pl.CostEstimate(flops=int(2 * 1.15e9), bytes_accessed=1024, transcendentals=0),
        name="attend_back",
    )(slopes, triple, triple, triple, grad, far, *deps)


def add_up(values):
    total = values[0].astype(F32)
    for value in values[1:]:
        total = total + value.astype(F32)
    return total.astype(BF16)


class Reduction:
    def __init__(self, pairs, d, dims, deps=()):
        self.pairs = [(left, right if right.ndim == 3 else right[None]) for left, right in pairs]
        self.d = d
        self.dims = dims
        self.sent, self.token = gradient_blocks(self.pairs, d, dims, deps=deps)

    def share(self):
        return flip(self.sent, 1)

    def own(self, got, deps=(), others=()):
        pairs = self.pairs + [pair for other, _ in others for pair in other.pairs]
        gots = [got] + [arrived for _, arrived in others]
        *self.parts, self.token = gradient_blocks(pairs, self.d, self.dims, gots, deps)

    def near(self):
        parts = self.parts
        return [flip(parts[0], 1 << self.dims[0]), flip(parts[2], 1 << self.dims[-1])]

    def near_landed(self, got):
        self.halves = []
        for side, order in ((0, self.dims), (1, self.dims[::-1])):
            stay = self.parts[2 * side + 1]
            left = [bit for bit in self.dims if bit != order[0]]
            shape = (2,) * len(left) + stay.shape[1:]
            values = [stay.reshape(shape), got[side].reshape(shape)]
            self.halves.append((values, list(order[1:]), left))

    def step(self):
        sends, self.stays = [], []
        for values, order, left in self.halves:
            at = left.index(order[0])
            sends.append(add_up([lax.index_in_dim(v, 1, at, keepdims=False) for v in values]))
            self.stays.append([lax.index_in_dim(v, 0, at, keepdims=False) for v in values])
        bits = [order[0] for _, order, _ in self.halves]
        return [flip(sends[0], 1 << bits[0]), flip(sends[1], 1 << bits[1])]

    def landed(self, got):
        halves = []
        for i, (_, order, left) in enumerate(self.halves):
            halves.append((self.stays[i] + [got[i]], order[1:], [b for b in left if b != order[0]]))
        self.halves = halves

    def cross(self):
        while len(self.halves[0][1]) > 1:
            self.landed(self.step())
        return self.step()

    def rows(self):
        self.value = jnp.concatenate([add_up(values) for values, _, _ in self.halves], axis=1)
        self.stage = 0
        return self.value

    def along(self):
        rep = lax.axis_size("rep")
        half = rep // 2
        k = self.stage
        if k < half - 1:
            pairs = [(k, k + 1), (rep - 1 - k, rep - 2 - k)]
        elif k == half - 1:
            pairs = [(k, k + 1), (k + 1, k)]
        else:
            i = rep - 2 - k
            pairs = [(i + 1, i), (rep - 2 - i, rep - 1 - i)]
        return lax.ppermute(self.value, "rep", pairs)

    def along_landed(self, got):
        rep = lax.axis_size("rep")
        z = lax.axis_index("rep")
        k = self.stage
        self.stage += 1
        if k < rep // 2:
            self.value = add_up([self.value, got])
        else:
            i = rep - 2 - k
            self.value = jnp.where((z == i) | (z == rep - 1 - i), got, self.value)

    def finish(self):
        while self.stage < lax.axis_size("rep") - 1:
            self.along_landed(self.along())
        return self.value.astype(F32)


class RepSum:
    def __init__(self, value):
        self.value = value
        self.bits = lax.axis_size("rep").bit_length() - 1
        self.steps = 2 * self.bits
        self.done = 0

    def mine(self):
        k = self.done
        bit = k if k < self.bits else self.steps - 1 - k
        z = lax.axis_index("rep")
        return bit, lax.bitwise_and(lax.shift_right_logical(z, bit), 1)

    def send(self):
        bit, mine = self.mine()
        if self.done >= self.bits:
            return rep_flip(self.value, 1 << bit)
        size = self.value.shape[0] // 2
        sent = lax.dynamic_slice_in_dim(self.value, (1 - mine) * size, size, 0)
        self.keep = lax.dynamic_slice_in_dim(self.value, mine * size, size, 0)
        return rep_flip(sent, 1 << bit)

    def landed(self, got):
        _, mine = self.mine()
        if self.done < self.bits:
            self.value = add_up([self.keep, got])
        else:
            lower = jnp.where(mine == 0, self.value, got)
            upper = jnp.where(mine == 0, got, self.value)
            self.value = jnp.concatenate([lower, upper], axis=0)
        self.done += 1


def nt(left, right):
    return lax.dot_general(left, right, (((1,), (1,)), ((), ())), preferred_element_type=F32)


def hidden_gradient(grad_result, w_down, slope, deps=()):
    total, width = grad_result.shape
    units = w_down.shape[0]
    tile = 512

    def body(grad_ref, w_ref, slope_ref, *refs):
        out_ref, sum_ref = refs[-2:]
        value = nt(grad_ref[...], w_ref[...]) * slope_ref[...].astype(F32)
        out_ref[...] = value.astype(BF16)
        sum_ref[...] = jnp.sum(value, axis=0, keepdims=True)

    return pl.pallas_call(
        body,
        out_shape=[
            jax.ShapeDtypeStruct((total, units), BF16),
            jax.ShapeDtypeStruct((1, units), F32),
        ],
        grid=(units // tile,),
        in_specs=[
            pl.BlockSpec((total, width), lambda c: (0, 0)),
            pl.BlockSpec((tile, width), lambda c: (c, 0)),
            pl.BlockSpec((total, tile), lambda c: (0, c)),
        ]
        + [ANY] * len(deps),
        out_specs=[
            pl.BlockSpec((total, tile), lambda c: (0, c)),
            pl.BlockSpec((1, tile), lambda c: (0, c)),
        ],
        compiler_params=pltpu.CompilerParams(vmem_limit_bytes=24 * 2**20),
        cost_estimate=pl.CostEstimate(flops=int(3 * 1.15e9), bytes_accessed=1024, transcendentals=0),
        name="hidden_gradient",
    )(grad_result, w_down, slope, *deps)


def mixed_gradient(hidden_low, w_up, w_out, mixed, grad_result, gain, deps=()):
    total, units = hidden_low.shape
    width = w_up.shape[0]
    tile = 256

    def body(low_ref, up_ref, out_w_ref, mixed_ref, result_ref, gain_ref, *outs):
        grad_ref, rounded_ref, attended_ref, sums_ref = outs[-4:]
        grad = nt(low_ref[...], up_ref[...])
        unit, scale = norm_parts(mixed_ref[...])
        result = result_ref[...].astype(F32)
        value = result + norm_back(grad, gain_ref[...], unit, scale)
        rounded = value.astype(BF16)
        grad_ref[...] = value
        rounded_ref[...] = rounded
        attended_ref[...] = nt(rounded, out_w_ref[...]).astype(BF16)

        @pl.when(pl.program_id(0) == 0)
        def _():
            sums_ref[...] = jnp.zeros_like(sums_ref)

        for i, terms in enumerate((value, grad * unit, grad, result)):
            sums_ref[pl.ds(i, 1), :] += jnp.sum(terms, axis=0, keepdims=True)

    rows = pl.BlockSpec((tile, width), lambda r: (r, 0))
    whole = [
        pl.BlockSpec((width, units), lambda r: (0, 0)),
        pl.BlockSpec((width, width), lambda r: (0, 0)),
    ]
    return pl.pallas_call(
        body,
        out_shape=[
            jax.ShapeDtypeStruct((total, width), F32),
            jax.ShapeDtypeStruct((total, width), BF16),
            jax.ShapeDtypeStruct((total, width), BF16),
            jax.ShapeDtypeStruct((8, width), F32),
        ],
        grid=(total // tile,),
        in_specs=[pl.BlockSpec((tile, units), lambda r: (r, 0))]
        + whole
        + [rows, rows, pl.BlockSpec((1, width), lambda r: (0, 0))]
        + [ANY] * len(deps),
        out_specs=[rows, rows, rows, pl.BlockSpec((8, width), lambda r: (0, 0))],
        compiler_params=pltpu.CompilerParams(vmem_limit_bytes=44 * 2**20),
        cost_estimate=pl.CostEstimate(flops=int(2 * 1.15e9), bytes_accessed=1024, transcendentals=0),
        name="mixed_gradient",
    )(hidden_low, w_up, w_out, mixed, grad_result, gain.reshape(1, width), *deps)


def normed_gradient(grad_triple, w_qkv, deps=()):
    three, total, width = grad_triple.shape
    tile = 256

    def body(grad_ref, w_ref, *refs):
        out_ref = refs[-1]
        value = nt(grad_ref[0], w_ref[:, pl.ds(0, width)])
        for i in range(1, three):
            value += nt(grad_ref[i], w_ref[:, pl.ds(i * width, width)])
        out_ref[...] = value.astype(BF16)

    return pl.pallas_call(
        body,
        out_shape=jax.ShapeDtypeStruct((total, width), BF16),
        grid=(total // tile,),
        in_specs=[
            pl.BlockSpec((three, tile, width), lambda r: (0, r, 0)),
            pl.BlockSpec((width, three * width), lambda r: (0, 0)),
        ]
        + [ANY] * len(deps),
        out_specs=pl.BlockSpec((tile, width), lambda r: (r, 0)),
        compiler_params=pltpu.CompilerParams(vmem_limit_bytes=24 * 2**20),
        cost_estimate=pl.CostEstimate(flops=int(2 * 1.15e9), bytes_accessed=1024, transcendentals=0),
        name="normed_gradient",
    )(grad_triple, w_qkv, *deps)


def matmul(left, right):
    return jnp.dot(left, right, preferred_element_type=F32)


def matmul_nt(left, right):
    return lax.dot_general(left, right, (((1,), (1,)), ((), ())), preferred_element_type=F32)


def matmul_tn(left, right):
    return lax.dot_general(left, right, (((0,), (0,)), ((), ())), preferred_element_type=F32)


def norm_parts(values):
    average = jnp.mean(values, axis=-1, keepdims=True)
    centred = values - average
    spread = jnp.mean(centred * centred, axis=-1, keepdims=True)
    scale = lax.rsqrt(spread + EPS)
    return centred * scale, scale


def norm_back(grad, gain, unit, scale):
    e = grad * gain
    return scale * (
        e
        - jnp.mean(e, axis=-1, keepdims=True)
        - unit * jnp.mean(e * unit, axis=-1, keepdims=True)
    )


def shards(
    inputs,
    skips,
    cotangent,
    dest_slot,
    pack_segments,
    block_live,
    counts,
    w_skip,
    b_skip,
    g_one,
    b_one,
    w_qkv,
    w_out,
    b_out,
    g_two,
    b_two,
    w_up,
    c_up,
    w_down,
    c_down,
):
    dp = lax.axis_size("dp")
    rep = lax.axis_size("rep")
    d = lax.axis_index("dp")
    z = lax.axis_index("rep")
    micro = inputs.shape[0]
    frames = inputs.shape[2]
    width = inputs.shape[3]
    blocks = dest_slot.shape[2]
    block = frames // blocks
    per_pair = blocks // dp
    total = micro * frames
    bits = dp.bit_length() - 1
    place = jnp.stack([z, lax.rem(d, 8)]).astype(jnp.int32)
    dims = list(range(1, bits))
    small = jnp.concatenate([dest_slot.reshape(-1), block_live.reshape(-1), counts.reshape(-1)])

    own_skip = own_chunk(place, width, [w_skip])
    own_skip, small = together(own_skip, small)
    z_skip = Fetch(own_skip)
    z_skip.rest()
    got = z_skip.send()
    every = small[None]
    for bit in range(bits):
        every = jnp.concatenate([every, flip(every, 1 << bit)], axis=0)
    z_mid = Fetch(own_chunk(place, width, [w_qkv, w_out], z_skip.held[1:]))
    z_mid.rest()
    z_skip.landed(got)

    run_skip = Spread(z_skip.far(), width, [every, z_mid.held[-1]])
    mid = z_mid.send()
    run_skip.near_landed(run_skip.near())

    span = micro * blocks
    numbers = every[:, : 2 * span].reshape(dp, 2 * micro, blocks)
    numbers = jnp.transpose(numbers, (1, 0, 2)).reshape(2 * micro, dp * blocks).astype(F32)
    count_total = jnp.sum(every[:, 2 * span]).astype(F32).reshape(1, 1)
    inner = jnp.arange(frames) % block
    live = inner[None] < jnp.repeat(block_live[:, 0, :], block, axis=1)
    codes = (2 * pack_segments[:, 0, :] + live).astype(F32)
    joined = jnp.concatenate([inputs.reshape(total, width), skips.reshape(total, width)], axis=1)
    far, far_turned, keep_wide, shuffle = plan_order(
        numbers[:micro], numbers[micro:], codes, d, block, [run_skip.pairs[0], joined]
    )
    keep_rows = keep_wide[:, :1]

    run_skip.cross_landed(run_skip.cross(), [shuffle, mid])

    z_mid.landed(mid)
    run_mid = Spread(z_mid.far(), width)
    full_skip, _ = assemble(
        w_skip, run_skip.parts(run_skip.share()), place, 0, 1, [run_mid.start[0]]
    )
    z_up = Fetch(own_chunk(place, width, [w_up], [run_mid.start[0]]))
    z_up.rest()
    base = matmul(joined, full_skip) + b_skip
    unit_one, scale_one = norm_parts(base)
    own_normed = (unit_one * g_one + b_one).astype(BF16)
    sent = matmul(shuffle, own_normed).astype(BF16)
    run_mid.near_landed(run_mid.near(), [sent, z_up.held[-1]])

    def exchange(values):
        values = values.reshape(dp, total // dp, width)
        got = lax.all_to_all(values, "dp", split_axis=0, concat_axis=0, tiled=True)
        return got.reshape(total, width)

    normed = exchange(sent)
    up = z_up.send([sent])
    z_down = Fetch(own_chunk(place, width, [w_down], [z_up.held[-1], sent]))
    z_down.rest()
    run_mid.cross_landed(run_mid.cross(), [up, z_down.held[-1], normed])
    z_up.landed(up)

    other = run_mid.share()
    run_up = Spread(z_up.far(), width, [run_mid.every])
    run_up.near_landed(run_up.near(), [other])
    shard_rows = w_qkv.shape[0] // 8
    parts_mid = run_mid.parts(other)
    full_qkv, _ = assemble(w_qkv, parts_mid, place, 0, 3)

    triple = matmul(normed, full_qkv).astype(BF16)
    triple = triple.reshape(dp, micro, per_pair * block, 3 * width)
    slopes = 2.0 ** (-8.0 * (jnp.arange(HEADS, dtype=F32) + 1.0) / HEADS)
    attended = attend(triple, far, slopes, [run_up.pairs[0]])
    down = z_down.send()
    run_up.cross_landed(run_up.cross(), [attended, down])
    z_down.landed(down)

    attended = exchange(attended)
    other = run_up.share()
    run_down = Spread(z_down.far(), width, [run_up.every])
    down = run_down.near()
    full_out, out_token = assemble(w_out, parts_mid, place, 3 * shard_rows, 1, [run_up.every])
    full_up, up_token = assemble(w_up, run_up.parts(other), place, 0, w_up.shape[1] // width)
    attended, out_token, up_token = together(attended, out_token, up_token)

    attended = matmul_tn(shuffle, attended).astype(BF16)
    mixed = base + matmul(attended, full_out) + (b_out + out_token[0, 0])
    unit_two, scale_two = norm_parts(mixed)
    normed_two = (unit_two * g_two + b_two).astype(BF16)
    count_total = count_total + up_token[:1, :1]
    for step in rep_steps(rep):
        count_total = count_total + rep_flip(count_total, step)
    share = counts[0, 0].astype(F32) * (dp * rep) / count_total[0, 0]
    run_down.near_landed(down, [up_token])
    down = run_down.cross()
    hidden = matmul(normed_two, full_up) + (c_up + run_down.token[0, 0])
    phi = 0.5 * (1.0 + lax.erf(hidden * (0.5**0.5)))
    active = (hidden * phi).astype(BF16)
    slope = (phi + hidden * jnp.exp(-0.5 * hidden * hidden) * ((2 * jnp.pi) ** -0.5)).astype(BF16)
    scaled = (cotangent.reshape(total, width).astype(F32) * share).astype(BF16)
    grad_result = scaled * keep_rows.astype(BF16)
    red_down = Reduction([(active, grad_result)], d, dims)

    down_got = red_down.share()
    run_down.cross_landed(down, [red_down.sent])
    full_down, _ = assemble(w_down, run_down.parts(run_down.share()), place, 0, 1)

    hidden_low, sum_hidden = hidden_gradient(grad_result, full_down, slope)
    red_up = Reduction([(normed_two, hidden_low)], d, dims)
    up_got = red_up.share()
    red_down.own(down_got, [red_up.sent])
    flying = red_down.near()
    grad_mixed, mixed_low, grad_attended, sums_mixed = mixed_gradient(
        hidden_low, full_up, full_out, mixed, grad_result, g_two, [red_down.token]
    )
    red_out = Reduction([(attended, mixed_low)], d, dims)
    out_got = red_out.share()
    flying, sums_mixed = together(flying, sums_mixed)
    red_down.near_landed(flying)

    down_flying = red_down.cross()
    sent = matmul(shuffle, grad_attended).astype(BF16)
    grad_attended = exchange(sent)
    red_up.own(up_got, [sent], [(red_out, out_got)])
    flying = red_up.near()
    down_flying, token = together(down_flying, red_up.token)
    red_down.landed(down_flying)
    red_down.rows()

    line = red_down.along()
    grad_attended = grad_attended.reshape(dp, micro, per_pair * block, width)
    grad_triple, token = attend_back(
        triple, grad_attended, far_turned, slopes, [red_down.value, token]
    )
    grad_triple = grad_triple.reshape(3, total, width)

    sent = normed_gradient(grad_triple, full_qkv)
    grad_normed = exchange(sent)
    flying, line, token = together(flying, line, token)
    red_mid = Reduction([(normed, grad_triple)], d, dims, [sent, token])
    grad_normed, token = together(grad_normed, red_mid.token)
    red_up.near_landed(flying)
    red_down.along_landed(line)
    up_flying = red_up.cross()
    line = red_down.along()

    mid_got = red_mid.share()
    grad_normed = matmul_tn(shuffle, grad_normed)
    grad_base = grad_mixed + norm_back(grad_normed, g_one, unit_one, scale_one)
    base_low = grad_base.astype(BF16)
    red_skip = Reduction([(joined, base_low)], d, dims, [token])
    skip_got = red_skip.share()
    vectors = (
        jnp.sum(grad_base, axis=0),
        jnp.sum(grad_normed * unit_one, axis=0),
        jnp.sum(grad_normed, axis=0),
        sums_mixed[0],
        sums_mixed[1],
        sums_mixed[2],
        sum_hidden[0],
        sums_mixed[3],
    )
    lengths = [v.shape[0] for v in vectors]
    summed = jnp.concatenate(vectors).reshape(-1, 128)
    for bit in range(bits - 1):
        summed = summed + flip(summed, 1 << bit)
    up_flying, token = together(up_flying, red_skip.token)
    red_up.landed(up_flying)
    red_up.rows()
    up_line = red_up.along()
    red_mid.own(mid_got, [token])
    summed, token = together(summed, red_mid.token)

    flying = red_mid.near()
    red_skip.own(skip_got, [token])
    skip_flying = red_skip.near()
    line, token = together(line, red_skip.token)
    red_down.along_landed(line)
    line = red_down.along()
    result = mixed + matmul(active, full_down) + (c_down + token[0, 0])
    output = (result * keep_rows).astype(BF16)
    grad_joined = matmul_nt(base_low, full_skip).astype(BF16)
    flying, up_line, grad_joined, summed = together(flying, up_line, grad_joined, summed)
    red_mid.near_landed(flying)
    red_up.along_landed(up_line)

    flying = red_mid.cross()
    up_line = red_up.along()
    flying, line, skip_flying, summed = together(flying, line, skip_flying, summed)
    red_down.along_landed(line)
    red_skip.near_landed(skip_flying)
    red_mid.landed(flying)

    mid_sum = RepSum(red_mid.rows())
    skip_flying = red_skip.cross()
    got = mid_sum.send()
    last = flip(summed, 1 << (bits - 1))
    got, up_line, skip_flying, last = together(got, up_line, skip_flying, last)
    mid_sum.landed(got)
    red_up.along_landed(up_line)
    red_skip.landed(skip_flying)
    summed = summed + last
    up_line = red_up.along()
    skip_columns = w_skip.shape[1]
    extra = jnp.pad(summed.reshape(-1), (0, -summed.size % (16 * rep * skip_columns)))
    extra = extra.reshape(-1, skip_columns).astype(BF16)
    skip_sum = RepSum(jnp.concatenate([red_skip.rows(), extra], axis=0))
    while mid_sum.done < mid_sum.steps:
        mid_got, skip_got = mid_sum.send(), skip_sum.send()
        if mid_sum.done == 1:
            mid_got, skip_got, up_line = together(mid_got, skip_got, up_line)
        else:
            mid_got, skip_got = together(mid_got, skip_got)
        mid_sum.landed(mid_got)
        skip_sum.landed(skip_got)
    skip_sum.landed(skip_sum.send())
    red_up.along_landed(up_line)
    final_mid = mid_sum.value.astype(F32)
    final_skip = skip_sum.value.astype(F32)
    own_rows = w_skip.shape[0] * rep // dp
    summed = final_skip[own_rows:].reshape(-1)
    final_up = red_up.finish()
    units = c_up.shape[0]
    finals = [
        red_down.finish(),
        final_up[:, :units],
        final_up[:, units:],
        final_mid,
        final_skip[:own_rows],
    ]
    sums = []
    offset = 0
    for length in lengths:
        sums.append(summed[offset : offset + length])
        offset += length

    def as_owned(values):
        return values.reshape(inputs.shape)

    return (
        as_owned(output),
        as_owned(grad_joined[:, :width]),
        as_owned(grad_joined[:, width:]),
        finals[4],
        sums[0],
        sums[1],
        sums[2],
        finals[3],
        finals[2],
        sums[3],
        sums[4],
        sums[5],
        finals[1],
        sums[6],
        finals[0],
        sums[7],
    )


def solution(mesh):
    frames = P(None, "rep", "dp", None)
    slots = P(None, "rep", "dp")
    rows = P("rep", None)
    whole = P()
    in_specs = (
        (frames,) * 3
        + (slots,) * 3
        + (P("dp", "rep"), rows, whole, whole, whole, rows, rows)
        + (whole,) * 3
        + (rows, whole, rows, whole)
    )
    split = P("dp", None)
    out_specs = (
        (frames,) * 3
        + (split,)
        + (whole,) * 3
        + (split, split)
        + (whole,) * 3
        + (split, whole, split, whole)
    )
    return jax.shard_map(shards, mesh=mesh, in_specs=in_specs, out_specs=out_specs, check_vma=False)
```

profile of v0, /device:TPU:0, one launch (start us, length us, event | category | flops | bytes accessed | tf_op | source)
XLA Modules:
  0.0 524.7 jit_solution(12298683633638666554)
XLA Ops:
  7.2 3.7 collective-permute-start
  14.4 3.4 collective-permute-done.refs_1_.refs_2_.refs_0_
  20.3 3.4 collective-permute-start.5
  27.4 4.0 collective-permute-done.1.refs_1_
  31.4 4.2 collective-permute-done.5.refs_3_.refs_1_.refs_0_
  61.6 2.4 assemble.5
  64.1 2.4 add_reduce_fusion
  69.2 3.9 all-to-all-start
  73.0 2.3 collective-permute-done.14.refs_5_.refs_1_.refs_0_
  77.1 2.2 pack.22
  86.4 13.8 %collective-permute-done.18.refs_5_.refs_1_.refs_0_ = bf16[128,1024]{1,0:T(8,128)(2,1)S(1)} collective-permute-done((bf16[128,1024]{1,0:T(8,128)(2,1)S(1)}, bf16[128,1024]{1,0:T(8,128)(2,1)S(1)}, u32[]{:S(2)}, u32[]{:S(2)}) %collective-permute-start.18) | collective-permute-done | bytes 262176 | tf_op jit(solution)/shard_map/ppermute | solution.py:25
  101.9 2.3 collective-permute-done.15.refs_1_
  112.6 2.5 collective-permute-start.24
  118.8 4.6 assemble.6
  123.5 3.7 convolution_convert_fusion
  132.0 16.6 %attend.1.refs_4_ = bf16[8,2,32,1024]{3,2,1,0:T(8,128)(2,1)S(1)} custom-call(f32[16]{0:T(128)S(1)} %multiply_power_fusion.slope_ref, bf16[8,2,32,3072]{3,2,1,0:T(8,128)(2,1)S(1)} %bitcast.136, bf16[8,2,32,3072]{3,2,1,0:T(8,128)(2,1)S(1)} %bitcast.137, bf16[8,2,32,3072]{3,2,1,0:T(8,128)(2,1)S(1)} %bitcast.138, f32[2,256,256]{2,1,0:T(8,128)S(1)} %copy-done.83, ...), custom_call_target="tpu_custom_call" | custom-call | flops 9200000000 | bytes 1024 | tf_op jit(solution)/shard_map/attend/pallas_call | solution.py:511
  151.5 4.5 all-to-all-start.1
  167.7 5.2 assemble.8
  172.9 3.2 copy-done.8
  186.0 2.2 collective-permute-start.30
  189.3 9.0 %fusion.4 = (bf16[512,4096]{1,0:T(8,128)(2,1)}, bf16[512,4096]{1,0:T(8,128)(2,1)S(1)}) fusion(f32[4096]{0:T(1024)S(1)} %broadcast_add_fusion, bf16[512,1024]{1,0:T(8,128)(2,1)S(1)} %add_convert_fusion.4.refs_0_, bf16[1024,4096]{1,0:T(8,128)(2,1)S(1)} %bitcast.145), kind=kOutput, calls=%fused_computation.5 | convolution fusion | flops 4320133120 | bytes 17842176 | tf_op jit(solution)/shard_map/dot_general | solution.py:835
  198.9 2.6 collective-permute-start.31
  203.6 4.6 gradient.9
  209.9 8.6 %collective-permute-done.32.refs_1_ = bf16[3072,512]{1,0:T(8,128)(2,1)S(1)} collective-permute-done((bf16[3072,512]{1,0:T(8,128)(2,1)S(1)}, bf16[3072,512]{1,0:T(8,128)(2,1)S(1)}, u32[]{:S(2)}, u32[]{:S(2)}) %collective-permute-start.32) | collective-permute-done | bytes 3145760 | tf_op jit(solution)/shard_map/ppermute | solution.py:20
  218.6 2.5 assemble.9
  221.2 6.7 %hidden_gradient.1 = (bf16[512,4096]{1,0:T(8,128)(2,1)S(1)}, f32[1,4096]{1,0:T(1,128)S(1)}) custom-call(bf16[512,1024]{1,0:T(8,128)(2,1)S(1)} %bitcast_multiply_fusion.grad_ref.result_ref, bf16[4096,1024]{1,0:T(8,128)(2,1)S(1)} %get-tuple-element.174.w_ref, bf16[512,4096]{1,0:T(8,128)(2,1)S(1)} %copy-done.23), custom_call_target="tpu_custom_call" | custom-call | flops 3449999872 | bytes 1024 | tf_op jit(solution)/shard_map/hidden_gradient/pallas_call | solution.py:736
  227.9 6.5 %gradient.10 = (bf16[4,128,4096]{2,1,0:T(8,128)(2,1)}, f32[8,128]{1,0:T(8,128)}) custom-call(s32[1]{0:T(128)} %bitcast.6.d_ref, bf16[512,1024]{1,0:T(8,128)(2,1)S(1)} %add_convert_fusion.4.refs_0_, bf16[1,512,4096]{2,1,0:T(8,128)(2,1)S(1)} %bitcast.142), custom_call_target="tpu_custom_call" | custom-call | flops 2875000064 | bytes 1024 | tf_op jit(solution)/shard_map/gradient/pallas_call | solution.py:452
  234.6 5.3 %gradient.11 = (bf16[2,512,512]{2,1,0:T(8,128)(2,1)}, bf16[2,512,512]{2,1,0:T(8,128)(2,1)S(1)}, bf16[2,512,512]{2,1,0:T(8,128)(2,1)}, bf16[2,512,512]{2,1,0:T(8,128)(2,1)S(1)}, f32[8,128]{1,0:T(8,128)S(1)}) custom-call(s32[1]{0:T(128)} %bitcast.6.d_ref, bf16[512,4096]{1,0:T(8,128)(2,1)S(1)} %get-tuple-element.291.refs_0_, ...), custom_call_target="tpu_custom_call" | custom-call | flops 2875000064 | bytes 1024 | tf_op jit(solution)/shard_map/gradient/pallas_call | solution.py:452
  244.6 11.4 %mixed_gradient.1 = (f32[512,1024]{1,0:T(8,128)S(1)}, bf16[512,1024]{1,0:T(8,128)(2,1)S(1)}, bf16[512,1024]{1,0:T(8,128)(2,1)S(1)}, f32[8,1024]{1,0:T(8,128)S(1)}) custom-call(bf16[512,4096]{1,0:T(8,128)(2,1)} %copy-done.6, bf16[1024,4096]{1,0:T(8,128)(2,1)} %copy-done.8, bf16[1024,1024]{1,0:T(8,128)(2,1)S(1)} %copy-done.43, ...), custom_call_target="tpu_custom_call" | custom-call | flops 2300000000 | bytes 1024 | tf_op jit(solution)/shard_map/mixed_gradient/pallas_call | solution.py:787
  258.2 9.3 %collective-permute-done.34 = bf16[2,512,512]{2,1,0:T(8,128)(2,1)S(1)} collective-permute-done((bf16[2,512,512]{2,1,0:T(8,128)(2,1)}, bf16[2,512,512]{2,1,0:T(8,128)(2,1)S(1)}, u32[]{:S(2)}, u32[]{:S(2)}) %collective-permute-start.34) | collective-permute-done | bytes 1048608 | tf_op jit(solution)/shard_map/ppermute | solution.py:20
  274.4 4.2 all-to-all-start.2
  278.6 2.2 copy-done.7
  282.0 10.4 %gradient.13 = (bf16[2,128,2560]{2,1,0:T(8,128)(2,1)}, bf16[2,128,2560]{2,1,0:T(8,128)(2,1)S(1)}, bf16[2,128,2560]{2,1,0:T(8,128)(2,1)}, bf16[2,128,2560]{2,1,0:T(8,128)(2,1)S(1)}, f32[8,128]{1,0:T(8,128)S(1)}) custom-call(s32[1]{0:T(128)} %bitcast.6.d_ref, bf16[512,1024]{1,0:T(8,128)(2,1)S(1)} %add_convert_fusion.4.refs_0_, ...), custom_call_target="tpu_custom_call" | custom-call | flops 2875000064 | bytes 1024 | tf_op jit(solution)/shard_map/gradient/pallas_call | solution.py:452
  299.6 4.0 collective-permute-start.42
  304.7 20.4 %attend_back.1 = (bf16[3,8,2,32,1024]{4,3,2,1,0:T(8,128)(2,1)S(1)}, f32[8,128]{1,0:T(8,128)S(1)}) custom-call(f32[16]{0:T(128)S(1)} %multiply_power_fusion.slope_ref, bf16[8,2,32,3072]{3,2,1,0:T(8,128)(2,1)S(1)} %bitcast.139, bf16[8,2,32,3072]{3,2,1,0:T(8,128)(2,1)S(1)} %bitcast.140, bf16[8,2,32,3072]{3,2,1,0:T(8,128)(2,1)S(1)} %bitcast.141, ...), custom_call_target="tpu_custom_call" | custom-call | flops 2300000000 | bytes 1024 | tf_op jit(solution)/shard_map/attend_back/pallas_call | solution.py:573
  325.1 3.9 copy-done.17
  329.0 4.7 normed_gradient.1.refs_2_
  333.7 4.4 all-to-all-start.3
  338.4 2.6 add_convert_fusion.3
  344.5 3.5 gradient.14
  349.6 3.9 all-to-all-done.3
  353.6 3.3 multiply_reduce_fusion
  362.3 2.1 gradient.15
  365.0 8.2 %collective-permute-done.48 = bf16[128,2560]{1,0:T(8,128)(2,1)S(1)} collective-permute-done((bf16[128,2560]{1,0:T(8,128)(2,1)S(1)}, bf16[128,2560]{1,0:T(8,128)(2,1)S(1)}, u32[]{:S(2)}, u32[]{:S(2)}) %collective-permute-start.48) | collective-permute-done | bytes 655392 | tf_op jit(solution)/shard_map/ppermute | solution.py:20
  373.2 3.7 collective-permute-start.46
  381.5 3.7 convolution_convert_fusion.1
  385.3 4.2 gradient.16
  390.9 2.2 collective-permute-start.51
  400.1 8.8 %collective-permute-done.52 = bf16[128,5120]{1,0:T(8,128)(2,1)S(1)} collective-permute-done((bf16[128,5120]{1,0:T(8,128)(2,1)S(1)}, bf16[128,5120]{1,0:T(8,128)(2,1)S(1)}, u32[]{:S(2)}, u32[]{:S(2)}) %collective-permute-start.52) | collective-permute-done | bytes 1310752 | tf_op jit(solution)/shard_map/ppermute | solution.py:669
  414.2 7.0 %collective-permute-done.56 = bf16[2,256,512]{2,1,0:T(8,128)(2,1)S(1)} collective-permute-done((bf16[2,256,512]{2,1,0:T(8,128)(2,1)S(1)}, bf16[2,256,512]{2,1,0:T(8,128)(2,1)S(1)}, u32[]{:S(2)}, u32[]{:S(2)}) %collective-permute-start.56) | collective-permute-done | bytes 524320 | tf_op jit(solution)/shard_map/ppermute | solution.py:20
  423.7 5.7 %collective-permute-done.53 = bf16[128,1536]{1,0:T(8,128)(2,1)S(1)} collective-permute-done((bf16[128,1536]{1,0:T(8,128)(2,1)S(1)}, bf16[128,1536]{1,0:T(8,128)(2,1)S(1)}, u32[]{:S(2)}, u32[]{:S(2)}) %collective-permute-start.53) | collective-permute-done | bytes 393248 | tf_op jit(solution)/shard_map/ppermute | solution.py:20
  429.8 2.5 collective-permute-start.58
  432.8 2.3 collective-permute-start.61
  435.4 5.5 %multiply_convert_fusion.1 = bf16[512,1024]{1,0:T(8,128)(2,1)} fusion(f32[512,1024]{1,0:T(8,128)S(1)} %copy-done.5, bf16[512,4096]{1,0:T(8,128)(2,1)S(1)} %copy-done.26, bf16[4096,1024]{1,0:T(8,128)(2,1)S(1)} %bitcast.147, f32[512]{0:T(512)S(1)} %slice_reduce_fusion, f32[1024]{0:T(1024)S(1)} %broadcast_add_fusion.1), kind=kOutput, calls=%fused_computation.14 | convolution fusion | flops 4297064448 | bytes 15734784 | tf_op jit(solution)/shard_map/dot_general | solution.py:835
  446.4 6.8 %collective-permute-start.64 = (bf16[160,1024]{1,0:T(8,128)(2,1)S(1)}, bf16[160,1024]{1,0:T(8,128)(2,1)S(1)}, u32[]{:S(2)}, u32[]{:S(2)}) collective-permute-start(bf16[160,1024]{1,0:T(8,128)(2,1)S(1)} %constant_dynamic-slice_fusion.1), channel_id=1, source_target_pairs={{0,1},{1,0},{2,3},{3,2},{4,5},{5,4},{6,7},{7,6},{8,9},{9,8},{10,11... | collective-permute-start | bytes 983048 | tf_op jit(solution)/shard_map/ppermute | solution.py:25
  455.0 3.9 collective-permute-start.63
  460.4 4.4 collective-permute-done.63
  465.6 24.2 %collective-permute-done.65 = bf16[128,5120]{1,0:T(8,128)(2,1)S(1)} collective-permute-done((bf16[128,5120]{1,0:T(8,128)(2,1)S(1)}, bf16[128,5120]{1,0:T(8,128)(2,1)S(1)}, u32[]{:S(2)}, u32[]{:S(2)}) %collective-permute-start.65) | collective-permute-done | bytes 1310752 | tf_op jit(solution)/shard_map/ppermute | solution.py:669
  490.1 3.0 collective-permute-start.67
  494.6 7.3 %collective-permute-done.67 = bf16[80,1024]{1,0:T(8,128)(2,1)S(1)} collective-permute-done((bf16[80,1024]{1,0:T(8,128)(2,1)S(1)}, bf16[80,1024]{1,0:T(8,128)(2,1)S(1)}, u32[]{:S(2)}, u32[]{:S(2)}) %collective-permute-start.67) | collective-permute-done | bytes 163872 | tf_op jit(solution)/shard_map/ppermute | solution.py:25
  502.5 3.4 collective-permute-start.69
  508.4 4.2 collective-permute-done.69
  513.9 2.9 collective-permute-start.70
  518.2 3.6 collective-permute-done.70
  (512 shorter events, 174.4 us)
Async XLA Ops:
  7.2 10.6 %collective-permute-start = (bf16[64,1024]{1,0:T(8,128)(2,1)S(1)}, bf16[64,1024]{1,0:T(8,128)(2,1)S(1)}, u32[]{:S(2)}, u32[]{:S(2)}) collective-permute-start(bf16[64,1024]{1,0:T(8,128)(2,1)S(1)} %own_chunk.4.refs_0_), channel_id=1, source_target_pairs={{0,2},{1,3},{2,0},{3,1},{4,6},{5,7},{6,4},{7,5},{8,10},{9,11},{10,... | collective-permute-start | bytes 393224 | tf_op jit(solution)/shard_map/ppermute | solution.py:25
  10.9 12.8 %collective-permute-start.3 = (s32[2,129]{1,0:T(2,128)S(1)}, s32[2,129]{1,0:T(2,128)S(1)}, u32[]{:S(2)}, u32[]{:S(2)}) collective-permute-start(s32[2,129]{1,0:T(2,128)S(1)} %pad_add_fusion.2), channel_id=1, source_target_pairs={{0,8},{4,12},{8,0},{12,4},{16,24},{20,28},{24,16},{28,20},{1,9},{5... | collective-permute-start | bytes 3104 | tf_op jit(solution)/shard_map/ppermute | solution.py:20
  18.7 12.7 %collective-permute-start.1 = (bf16[128,1024]{1,0:T(8,128)(2,1)S(1)}, bf16[128,1024]{1,0:T(8,128)(2,1)S(1)}, u32[]{:S(2)}, u32[]{:S(2)}) collective-permute-start(bf16[128,1024]{1,0:T(8,128)(2,1)S(1)} %get-tuple-element.135), channel_id=1, source_target_pairs={{0,1},{1,0},{2,3},{3,2},{4,5},{5,4},{6,7},{7,6},{8,9},{9,8},{10,11... | collective-permute-start | bytes 786440 | tf_op jit(solution)/shard_map/ppermute | solution.py:25
  20.3 15.4 %collective-permute-start.5 = (bf16[128,1024]{1,0:T(8,128)(2,1)S(1)}, bf16[128,1024]{1,0:T(8,128)(2,1)S(1)}, u32[]{:S(2)}, u32[]{:S(2)}) collective-permute-start(bf16[128,1024]{1,0:T(8,128)(2,1)S(1)} %own_chunk.5.refs_0_), channel_id=1, source_target_pairs={{0,2},{1,3},{2,0},{3,1},{4,6},{5,7},{6,4},{7,5},{8,10},{9,11},{10,... | collective-permute-start | bytes 786440 | tf_op jit(solution)/shard_map/ppermute | solution.py:25
  40.3 12.8 %collective-permute-start.10 = (bf16[256,1024]{1,0:T(8,128)(2,1)}, bf16[256,1024]{1,0:T(8,128)(2,1)S(1)}, u32[]{:S(2)}, u32[]{:S(2)}) collective-permute-start(bf16[256,1024]{1,0:T(8,128)(2,1)} %get-tuple-element.142), channel_id=1, source_target_pairs={{0,1},{1,0},{2,3},{3,2},{4,5},{5,4},{6,7},{7,6},{8,9},{9,8},{10,11... | collective-permute-start | bytes 1572872 | tf_op jit(solution)/shard_map/ppermute | solution.py:25
  45.4 9.2 %collective-permute-start.8 = (bf16[384,512]{1,0:T(8,128)(2,1)S(1)}, bf16[384,512]{1,0:T(8,128)(2,1)}, u32[]{:S(2)}, u32[]{:S(2)}) collective-permute-start(bf16[384,512]{1,0:T(8,128)(2,1)S(1)} %get-tuple-element.139.refs_0_), channel_id=1, source_target_pairs={{0,16},{4,20},{8,24},{12,28},{16,0},{20,4},{24,8},{28,12},{1,17},{... | collective-permute-start | bytes 1179656 | tf_op jit(solution)/shard_map/ppermute | solution.py:20
  47.0 9.1 %collective-permute-start.9 = (bf16[384,512]{1,0:T(8,128)(2,1)}, bf16[384,512]{1,0:T(8,128)(2,1)}, u32[]{:S(2)}, u32[]{:S(2)}) collective-permute-start(bf16[384,512]{1,0:T(8,128)(2,1)} %get-tuple-element.140.refs_2_), channel_id=1, source_target_pairs={{0,8},{4,12},{8,0},{12,4},{16,24},{20,28},{24,16},{28,20},{1,9},{5... | collective-permute-start | bytes 1179656 | tf_op jit(solution)/shard_map/ppermute | solution.py:20
  59.0 16.3 %collective-permute-start.12 = (bf16[384,512]{1,0:T(8,128)(2,1)S(1)}, bf16[384,512]{1,0:T(8,128)(2,1)S(1)}, u32[]{:S(2)}, u32[]{:S(2)}) collective-permute-start(bf16[384,512]{1,0:T(8,128)(2,1)S(1)} %get-tuple-element.144.refs_2_.refs_1_.refs_0_), channel_id=1, source_target_pairs={{0,8},{4,12},{8,0},{12,4},{16,24},{20,28},{24,16},{28,20},{1,9},{5... | collective-permute-start | bytes 1179656 | tf_op jit(solution)/shard_map/ppermute | solution.py:20
  59.6 16.5 %collective-permute-start.13 = (bf16[384,512]{1,0:T(8,128)(2,1)S(1)}, bf16[384,512]{1,0:T(8,128)(2,1)}, u32[]{:S(2)}, u32[]{:S(2)}) collective-permute-start(bf16[384,512]{1,0:T(8,128)(2,1)S(1)} %get-tuple-element.146.refs_2_), channel_id=1, source_target_pairs={{0,16},{4,20},{8,24},{12,28},{16,0},{20,4},{24,8},{28,12},{1,17},{... | collective-permute-start | bytes 1179656 | tf_op jit(solution)/shard_map/ppermute | solution.py:20
  60.8 14.5 %collective-permute-start.14 = (bf16[128,1024]{1,0:T(8,128)(2,1)S(1)}, bf16[128,1024]{1,0:T(8,128)(2,1)S(1)}, u32[]{:S(2)}, u32[]{:S(2)}) collective-permute-start(bf16[128,1024]{1,0:T(8,128)(2,1)S(1)} %own_chunk.6.refs_0_), channel_id=1, source_target_pairs={{0,2},{1,3},{2,0},{3,1},{4,6},{5,7},{6,4},{7,5},{8,10},{9,11},{10,... | collective-permute-start | bytes 786440 | tf_op jit(solution)/shard_map/ppermute | solution.py:25
  69.2 36.9 %all-to-all-start = ((bf16[8,64,1024]{2,1,0:T(8,128)(2,1)}), bf16[8,64,1024]{2,1,0:T(8,128)(2,1)S(1)}, u32[]{:S(2)}, u32[]{:S(2)}) async-start(bf16[8,64,1024]{2,1,0:T(8,128)(2,1)} %bitcast.10), calls=%async_computation | async-start | bytes 2097152 | tf_op jit(solution)/shard_map/all_to_all | solution.py:947
  79.3 25.0 %collective-permute-start.15 = (bf16[768,512]{1,0:T(8,128)(2,1)S(1)}, bf16[768,512]{1,0:T(8,128)(2,1)S(1)}, u32[]{:S(2)}, u32[]{:S(2)}) collective-permute-start(bf16[768,512]{1,0:T(8,128)(2,1)S(1)} %get-tuple-element.147.refs_0_), channel_id=1, source_target_pairs={{0,16},{4,20},{8,24},{12,28},{16,0},{20,4},{24,8},{28,12},{1,17},{... | collective-permute-start | bytes 2359304 | tf_op jit(solution)/shard_map/ppermute | solution.py:20
  80.8 24.3 %collective-permute-start.16 = (bf16[768,512]{1,0:T(8,128)(2,1)S(1)}, bf16[768,512]{1,0:T(8,128)(2,1)S(1)}, u32[]{:S(2)}, u32[]{:S(2)}) collective-permute-start(bf16[768,512]{1,0:T(8,128)(2,1)S(1)} %get-tuple-element.148.refs_2_), channel_id=1, source_target_pairs={{0,8},{4,12},{8,0},{12,4},{16,24},{20,28},{24,16},{28,20},{1,9},{5... | collective-permute-start | bytes 2359304 | tf_op jit(solution)/shard_map/ppermute | solution.py:20
  83.0 19.0 %collective-permute-start.17 = (bf16[256,1024]{1,0:T(8,128)(2,1)S(1)}, bf16[256,1024]{1,0:T(8,128)(2,1)S(1)}, u32[]{:S(2)}, u32[]{:S(2)}) collective-permute-start(bf16[256,1024]{1,0:T(8,128)(2,1)S(1)} %get-tuple-element.149), channel_id=1, source_target_pairs={{0,1},{1,0},{2,3},{3,2},{4,5},{5,4},{6,7},{7,6},{8,9},{9,8},{10,11... | collective-permute-start | bytes 1572872 | tf_op jit(solution)/shard_map/ppermute | solution.py:25
  84.3 16.0 %collective-permute-start.18 = (bf16[128,1024]{1,0:T(8,128)(2,1)S(1)}, bf16[128,1024]{1,0:T(8,128)(2,1)S(1)}, u32[]{:S(2)}, u32[]{:S(2)}) collective-permute-start(bf16[128,1024]{1,0:T(8,128)(2,1)S(1)} %own_chunk.7.refs_0_), channel_id=1, source_target_pairs={{0,2},{1,3},{2,0},{3,1},{4,6},{5,7},{6,4},{7,5},{8,10},{9,11},{10,... | collective-permute-start | bytes 786440 | tf_op jit(solution)/shard_map/ppermute | solution.py:25
  112.6 36.0 %collective-permute-start.24 = (bf16[256,1024]{1,0:T(8,128)(2,1)S(1)}, bf16[256,1024]{1,0:T(8,128)(2,1)S(1)}, u32[]{:S(2)}, u32[]{:S(2)}) collective-permute-start(bf16[256,1024]{1,0:T(8,128)(2,1)S(1)} %get-tuple-element.157), channel_id=1, source_target_pairs={{0,1},{1,0},{2,3},{3,2},{4,5},{5,4},{6,7},{7,6},{8,9},{9,8},{10,11... | collective-permute-start | bytes 1572872 | tf_op jit(solution)/shard_map/ppermute | solution.py:25
  116.9 11.2 %collective-permute-start.20 = (bf16[384,512]{1,0:T(8,128)(2,1)S(1)}, bf16[384,512]{1,0:T(8,128)(2,1)S(1)}, u32[]{:S(2)}, u32[]{:S(2)}) collective-permute-start(bf16[384,512]{1,0:T(8,128)(2,1)S(1)} %get-tuple-element.153.refs_0_), channel_id=1, source_target_pairs={{0,8},{4,12},{8,0},{12,4},{16,24},{20,28},{24,16},{28,20},{1,9},{5... | collective-permute-start | bytes 1179656 | tf_op jit(solution)/shard_map/ppermute | solution.py:20
  118.4 10.9 %collective-permute-start.21 = (bf16[384,512]{1,0:T(8,128)(2,1)S(1)}, bf16[384,512]{1,0:T(8,128)(2,1)S(1)}, u32[]{:S(2)}, u32[]{:S(2)}) collective-permute-start(bf16[384,512]{1,0:T(8,128)(2,1)S(1)} %get-tuple-element.154.refs_2_), channel_id=1, source_target_pairs={{0,16},{4,20},{8,24},{12,28},{16,0},{20,4},{24,8},{28,12},{1,17},{... | collective-permute-start | bytes 1179656 | tf_op jit(solution)/shard_map/ppermute | solution.py:20
  130.7 18.6 %collective-permute-start.22 = (bf16[768,512]{1,0:T(8,128)(2,1)S(1)}, bf16[768,512]{1,0:T(8,128)(2,1)S(1)}, u32[]{:S(2)}, u32[]{:S(2)}) collective-permute-start(bf16[768,512]{1,0:T(8,128)(2,1)S(1)} %get-tuple-element.155.refs_0_), channel_id=1, source_target_pairs={{0,16},{4,20},{8,24},{12,28},{16,0},{20,4},{24,8},{28,12},{1,17},{... | collective-permute-start | bytes 2359304 | tf_op jit(solution)/shard_map/ppermute | solution.py:20
  131.2 18.2 %collective-permute-start.23 = (bf16[768,512]{1,0:T(8,128)(2,1)S(1)}, bf16[768,512]{1,0:T(8,128)(2,1)S(1)}, u32[]{:S(2)}, u32[]{:S(2)}) collective-permute-start(bf16[768,512]{1,0:T(8,128)(2,1)S(1)} %get-tuple-element.156.refs_2_), channel_id=1, source_target_pairs={{0,8},{4,12},{8,0},{12,4},{16,24},{20,28},{24,16},{28,20},{1,9},{5... | collective-permute-start | bytes 2359304 | tf_op jit(solution)/shard_map/ppermute | solution.py:20
  151.4 16.3 %collective-permute-start.25 = (bf16[3072,512]{1,0:T(8,128)(2,1)}, bf16[3072,512]{1,0:T(8,128)(2,1)}, u32[]{:S(2)}, u32[]{:S(2)}) collective-permute-start(bf16[3072,512]{1,0:T(8,128)(2,1)} %get-tuple-element.158.refs_2_.refs_0_), channel_id=1, source_target_pairs={{0,4},{4,0},{8,12},{12,8},{16,20},{20,16},{24,28},{28,24},{1,5},{5... | collective-permute-start | bytes 9437192 | tf_op jit(solution)/shard_map/ppermute | solution.py:20
  151.5 24.7 %all-to-all-start.1 = ((bf16[8,64,1024]{2,1,0:T(8,128)(2,1)}), bf16[8,64,1024]{2,1,0:T(8,128)(2,1)}, u32[]{:S(2)}, u32[]{:S(2)}) async-start(bf16[8,64,1024]{2,1,0:T(8,128)(2,1)} %bitcast.152), calls=%async_computation.1 | async-start | bytes 2097152 | tf_op jit(solution)/shard_map/all_to_all | solution.py:947
  161.1 18.2 %collective-permute-start.26 = (bf16[384,512]{1,0:T(8,128)(2,1)}, bf16[384,512]{1,0:T(8,128)(2,1)S(1)}, u32[]{:S(2)}, u32[]{:S(2)}) collective-permute-start(bf16[384,512]{1,0:T(8,128)(2,1)} %get-tuple-element.165.refs_0_), channel_id=1, source_target_pairs={{0,8},{4,12},{8,0},{12,4},{16,24},{20,28},{24,16},{28,20},{1,9},{5... | collective-permute-start | bytes 1179656 | tf_op jit(solution)/shard_map/ppermute | solution.py:20
  163.1 16.2 %collective-permute-start.27 = (bf16[384,512]{1,0:T(8,128)(2,1)}, bf16[384,512]{1,0:T(8,128)(2,1)}, u32[]{:S(2)}, u32[]{:S(2)}) collective-permute-start(bf16[384,512]{1,0:T(8,128)(2,1)} %get-tuple-element.166.refs_2_), channel_id=1, source_target_pairs={{0,16},{4,20},{8,24},{12,28},{16,0},{20,4},{24,8},{28,12},{1,17},{... | collective-permute-start | bytes 1179656 | tf_op jit(solution)/shard_map/ppermute | solution.py:20
  184.0 24.3 %collective-permute-start.28 = (bf16[768,512]{1,0:T(8,128)(2,1)S(1)}, bf16[768,512]{1,0:T(8,128)(2,1)S(1)}, u32[]{:S(2)}, u32[]{:S(2)}) collective-permute-start(bf16[768,512]{1,0:T(8,128)(2,1)S(1)} %get-tuple-element.169.refs_0_), channel_id=1, source_target_pairs={{0,16},{4,20},{8,24},{12,28},{16,0},{20,4},{24,8},{28,12},{1,17},{... | collective-permute-start | bytes 2359304 | tf_op jit(solution)/shard_map/ppermute | solution.py:20
  184.8 23.5 %collective-permute-start.29 = (bf16[768,512]{1,0:T(8,128)(2,1)S(1)}, bf16[768,512]{1,0:T(8,128)(2,1)S(1)}, u32[]{:S(2)}, u32[]{:S(2)}) collective-permute-start(bf16[768,512]{1,0:T(8,128)(2,1)S(1)} %get-tuple-element.170.refs_2_), channel_id=1, source_target_pairs={{0,8},{4,12},{8,0},{12,4},{16,24},{20,28},{24,16},{28,20},{1,9},{5... | collective-permute-start | bytes 2359304 | tf_op jit(solution)/shard_map/ppermute | solution.py:20
  186.0 12.3 %collective-permute-start.30 = (f32[1,1]{1,0:T(1,128)}, f32[1,1]{1,0:T(1,128)}, u32[]{:S(2)}, u32[]{:S(2)}) collective-permute-start(f32[1,1]{1,0:T(1,128)} %add.312), channel_id=1, source_target_pairs={{0,2},{1,3},{2,0},{3,1},{4,6},{5,7},{6,4},{7,5},{8,10},{9,11},{10,... | collective-permute-start | bytes 20 | tf_op jit(solution)/shard_map/ppermute | solution.py:25
  209.1 9.4 %collective-permute-start.32 = (bf16[3072,512]{1,0:T(8,128)(2,1)S(1)}, bf16[3072,512]{1,0:T(8,128)(2,1)S(1)}, u32[]{:S(2)}, u32[]{:S(2)}) collective-permute-start(bf16[3072,512]{1,0:T(8,128)(2,1)S(1)} %get-tuple-element.173.refs_0_), channel_id=1, source_target_pairs={{0,4},{4,0},{8,12},{12,8},{16,20},{20,16},{24,28},{28,24},{1,5},{5... | collective-permute-start | bytes 9437192 | tf_op jit(solution)/shard_map/ppermute | solution.py:20
  209.2 25.3 %collective-permute-start.33 = (bf16[4,512,1024]{2,1,0:T(8,128)(2,1)}, bf16[4,512,1024]{2,1,0:T(8,128)(2,1)S(1)}, u32[]{:S(2)}, u32[]{:S(2)}) collective-permute-start(bf16[4,512,1024]{2,1,0:T(8,128)(2,1)} %get-tuple-element.172.refs_4_), channel_id=1, source_target_pairs={{0,4},{4,0},{8,12},{12,8},{16,20},{20,16},{24,28},{28,24},{1,5},{5... | collective-permute-start | bytes 12582920 | tf_op jit(solution)/shard_map/ppermute | solution.py:20
  234.4 44.2 %collective-permute-start.38 = (bf16[4,128,4096]{2,1,0:T(8,128)(2,1)}, bf16[4,128,4096]{2,1,0:T(8,128)(2,1)}, u32[]{:S(2)}, u32[]{:S(2)}) collective-permute-start(bf16[4,128,4096]{2,1,0:T(8,128)(2,1)} %get-tuple-element.176.refs_3_), channel_id=1, source_target_pairs={{0,4},{4,0},{8,12},{12,8},{16,20},{20,16},{24,28},{28,24},{1,5},{5... | collective-permute-start | bytes 12582920 | tf_op jit(solution)/shard_map/ppermute | solution.py:20
  241.8 25.6 %collective-permute-start.34 = (bf16[2,512,512]{2,1,0:T(8,128)(2,1)}, bf16[2,512,512]{2,1,0:T(8,128)(2,1)S(1)}, u32[]{:S(2)}, u32[]{:S(2)}) collective-permute-start(bf16[2,512,512]{2,1,0:T(8,128)(2,1)} %get-tuple-element.178), channel_id=1, source_target_pairs={{0,8},{4,12},{8,0},{12,4},{16,24},{20,28},{24,16},{28,20},{1,9},{5... | collective-permute-start | bytes 3145736 | tf_op jit(solution)/shard_map/ppermute | solution.py:20
  243.3 25.3 %collective-permute-start.35 = (bf16[2,512,512]{2,1,0:T(8,128)(2,1)}, bf16[2,512,512]{2,1,0:T(8,128)(2,1)S(1)}, u32[]{:S(2)}, u32[]{:S(2)}) collective-permute-start(bf16[2,512,512]{2,1,0:T(8,128)(2,1)} %get-tuple-element.179), channel_id=1, source_target_pairs={{0,16},{4,20},{8,24},{12,28},{16,0},{20,4},{24,8},{28,12},{1,17},{... | collective-permute-start | bytes 3145736 | tf_op jit(solution)/shard_map/ppermute | solution.py:20
  258.1 20.5 %collective-permute-start.39 = (bf16[4,128,1024]{2,1,0:T(8,128)(2,1)}, bf16[4,128,1024]{2,1,0:T(8,128)(2,1)}, u32[]{:S(2)}, u32[]{:S(2)}) collective-permute-start(bf16[4,128,1024]{2,1,0:T(8,128)(2,1)} %get-tuple-element.186), channel_id=1, source_target_pairs={{0,4},{4,0},{8,12},{12,8},{16,20},{20,16},{24,28},{28,24},{1,5},{5... | collective-permute-start | bytes 3145736 | tf_op jit(solution)/shard_map/ppermute | solution.py:20
  269.7 26.1 %collective-permute-start.36 = (bf16[512,512]{1,0:T(8,128)(2,1)}, bf16[512,512]{1,0:T(8,128)(2,1)}, u32[]{:S(2)}, u32[]{:S(2)}) collective-permute-start(bf16[512,512]{1,0:T(8,128)(2,1)} %fusion.15), channel_id=1, source_target_pairs={{0,16},{4,20},{8,24},{12,28},{16,0},{20,4},{24,8},{28,12},{1,17},{... | collective-permute-start | bytes 1572872 | tf_op jit(solution)/shard_map/ppermute | solution.py:20
  271.9 23.9 %collective-permute-start.37 = (bf16[512,512]{1,0:T(8,128)(2,1)}, bf16[512,512]{1,0:T(8,128)(2,1)}, u32[]{:S(2)}, u32[]{:S(2)}) collective-permute-start(bf16[512,512]{1,0:T(8,128)(2,1)} %fusion.16), channel_id=1, source_target_pairs={{0,8},{4,12},{8,0},{12,4},{16,24},{20,28},{24,16},{28,20},{1,9},{5... | collective-permute-start | bytes 1572872 | tf_op jit(solution)/shard_map/ppermute | solution.py:20
  274.4 29.3 %all-to-all-start.2 = ((bf16[8,64,1024]{2,1,0:T(8,128)(2,1)}), bf16[8,64,1024]{2,1,0:T(8,128)(2,1)}, u32[]{:S(2)}, u32[]{:S(2)}) async-start(bf16[8,64,1024]{2,1,0:T(8,128)(2,1)} %bitcast.28), calls=%async_computation.2 | async-start | bytes 2097152 | tf_op jit(solution)/shard_map/all_to_all | solution.py:947
  292.4 45.9 %collective-permute-start.40 = (bf16[2,128,2560]{2,1,0:T(8,128)(2,1)}, bf16[2,128,2560]{2,1,0:T(8,128)(2,1)}, u32[]{:S(2)}, u32[]{:S(2)}) collective-permute-start(bf16[2,128,2560]{2,1,0:T(8,128)(2,1)} %get-tuple-element.191), channel_id=1, source_target_pairs={{0,8},{4,12},{8,0},{12,4},{16,24},{20,28},{24,16},{28,20},{1,9},{5... | collective-permute-start | bytes 3932168 | tf_op jit(solution)/shard_map/ppermute | solution.py:20
  294.3 44.0 %collective-permute-start.41 = (bf16[2,128,2560]{2,1,0:T(8,128)(2,1)}, bf16[2,128,2560]{2,1,0:T(8,128)(2,1)}, u32[]{:S(2)}, u32[]{:S(2)}) collective-permute-start(bf16[2,128,2560]{2,1,0:T(8,128)(2,1)} %get-tuple-element.192), channel_id=1, source_target_pairs={{0,16},{4,20},{8,24},{12,28},{16,0},{20,4},{24,8},{28,12},{1,17},{... | collective-permute-start | bytes 3932168 | tf_op jit(solution)/shard_map/ppermute | solution.py:20
  299.6 38.7 %collective-permute-start.42 = (bf16[512,1024]{1,0:T(8,128)(2,1)}, bf16[512,1024]{1,0:T(8,128)(2,1)}, u32[]{:S(2)}, u32[]{:S(2)}) collective-permute-start(bf16[512,1024]{1,0:T(8,128)(2,1)} %pad_maximum_fusion.2.refs_0_), channel_id=1, source_target_pairs={{0,1},{3,2},{4,5},{7,6},{8,9},{11,10},{12,13},{15,14},{16,17},{19,... | collective-permute-start | bytes 3145736 | tf_op jit(solution)/shard_map/ppermute | solution.py:669
  333.7 19.8 %all-to-all-start.3 = ((bf16[8,64,1024]{2,1,0:T(8,128)(2,1)}), bf16[8,64,1024]{2,1,0:T(8,128)(2,1)}, u32[]{:S(2)}, u32[]{:S(2)}) async-start(bf16[8,64,1024]{2,1,0:T(8,128)(2,1)} %bitcast.31), calls=%async_computation.3 | async-start | bytes 2097152 | tf_op jit(solution)/shard_map/all_to_all | solution.py:947
  340.9 54.2 %collective-permute-start.43 = (bf16[512,1024]{1,0:T(8,128)(2,1)}, bf16[512,1024]{1,0:T(8,128)(2,1)}, u32[]{:S(2)}, u32[]{:S(2)}) collective-permute-start(bf16[512,1024]{1,0:T(8,128)(2,1)} %add_convert_fusion.3), channel_id=1, source_target_pairs={{1,2},{2,1},{5,6},{6,5},{9,10},{10,9},{13,14},{14,13},{17,18},{18,... | collective-permute-start | bytes 3145736 | tf_op jit(solution)/shard_map/ppermute | solution.py:669
  359.6 13.6 %collective-permute-start.48 = (bf16[128,2560]{1,0:T(8,128)(2,1)S(1)}, bf16[128,2560]{1,0:T(8,128)(2,1)S(1)}, u32[]{:S(2)}, u32[]{:S(2)}) collective-permute-start(bf16[128,2560]{1,0:T(8,128)(2,1)S(1)} %fusion.13), channel_id=1, source_target_pairs={{0,16},{4,20},{8,24},{12,28},{16,0},{20,4},{24,8},{28,12},{1,17},{... | collective-permute-start | bytes 1966088 | tf_op jit(solution)/shard_map/ppermute | solution.py:20
  361.5 15.4 %collective-permute-start.49 = (bf16[128,2560]{1,0:T(8,128)(2,1)S(1)}, bf16[128,2560]{1,0:T(8,128)(2,1)S(1)}, u32[]{:S(2)}, u32[]{:S(2)}) collective-permute-start(bf16[128,2560]{1,0:T(8,128)(2,1)S(1)} %fusion.14), channel_id=1, source_target_pairs={{0,8},{4,12},{8,0},{12,4},{16,24},{20,28},{24,16},{28,20},{1,9},{5... | collective-permute-start | bytes 1966088 | tf_op jit(solution)/shard_map/ppermute | solution.py:20
  364.4 28.6 %collective-permute-start.44 = (bf16[4,256,1024]{2,1,0:T(8,128)(2,1)S(1)}, bf16[4,256,1024]{2,1,0:T(8,128)(2,1)S(1)}, u32[]{:S(2)}, u32[]{:S(2)}) collective-permute-start(bf16[4,256,1024]{2,1,0:T(8,128)(2,1)S(1)} %get-tuple-element.203), channel_id=1, source_target_pairs={{0,4},{4,0},{8,12},{12,8},{16,20},{20,16},{24,28},{28,24},{1,5},{5... | collective-permute-start | bytes 6291464 | tf_op jit(solution)/shard_map/ppermute | solution.py:20
  364.9 20.3 %collective-permute-start.47 = (bf16[4,128,3072]{2,1,0:T(8,128)(2,1)S(1)}, bf16[4,128,3072]{2,1,0:T(8,128)(2,1)S(1)}, u32[]{:S(2)}, u32[]{:S(2)}) collective-permute-start(bf16[4,128,3072]{2,1,0:T(8,128)(2,1)S(1)} %copy-done.81), channel_id=1, source_target_pairs={{0,4},{4,0},{8,12},{12,8},{16,20},{20,16},{24,28},{28,24},{1,5},{5... | collective-permute-start | bytes 9437192 | tf_op jit(solution)/shard_map/ppermute | solution.py:20
  373.2 12.0 %collective-permute-start.46 = (f32[88,128]{1,0:T(8,128)S(1)}, f32[88,128]{1,0:T(8,128)S(1)}, u32[]{:S(2)}, u32[]{:S(2)}) collective-permute-start(f32[88,128]{1,0:T(8,128)S(1)} %bitcast_add_fusion.8), channel_id=1, source_target_pairs={{0,8},{4,12},{8,0},{12,4},{16,24},{20,28},{24,16},{28,20},{1,9},{5... | collective-permute-start | bytes 135176 | tf_op jit(solution)/shard_map/ppermute | solution.py:20
  379.9 29.0 %collective-permute-start.52 = (bf16[128,5120]{1,0:T(8,128)(2,1)S(1)}, bf16[128,5120]{1,0:T(8,128)(2,1)S(1)}, u32[]{:S(2)}, u32[]{:S(2)}) collective-permute-start(bf16[128,5120]{1,0:T(8,128)(2,1)S(1)} %pad_maximum_fusion.1), channel_id=1, source_target_pairs={{0,1},{3,2},{4,5},{7,6},{8,9},{11,10},{12,13},{15,14},{16,17},{19,... | collective-permute-start | bytes 3932168 | tf_op jit(solution)/shard_map/ppermute | solution.py:669
  389.4 20.5 %collective-permute-start.50 = (bf16[2,128,1536]{2,1,0:T(8,128)(2,1)S(1)}, bf16[2,128,1536]{2,1,0:T(8,128)(2,1)S(1)}, u32[]{:S(2)}, u32[]{:S(2)}) collective-permute-start(bf16[2,128,1536]{2,1,0:T(8,128)(2,1)S(1)} %get-tuple-element.217), channel_id=1, source_target_pairs={{0,8},{4,12},{8,0},{12,4},{16,24},{20,28},{24,16},{28,20},{1,9},{5... | collective-permute-start | bytes 2359304 | tf_op jit(solution)/shard_map/ppermute | solution.py:20
  390.9 19.1 %collective-permute-start.51 = (bf16[2,128,1536]{2,1,0:T(8,128)(2,1)S(1)}, bf16[2,128,1536]{2,1,0:T(8,128)(2,1)S(1)}, u32[]{:S(2)}, u32[]{:S(2)}) collective-permute-start(bf16[2,128,1536]{2,1,0:T(8,128)(2,1)S(1)} %get-tuple-element.218), channel_id=1, source_target_pairs={{0,16},{4,20},{8,24},{12,28},{16,0},{20,4},{24,8},{28,12},{1,17},{... | collective-permute-start | bytes 2359304 | tf_op jit(solution)/shard_map/ppermute | solution.py:20
  397.7 26.0 %collective-permute-start.55 = (bf16[512,1024]{1,0:T(8,128)(2,1)S(1)}, bf16[512,1024]{1,0:T(8,128)(2,1)S(1)}, u32[]{:S(2)}, u32[]{:S(2)}) collective-permute-start(bf16[512,1024]{1,0:T(8,128)(2,1)S(1)} %add_convert_fusion.2), channel_id=1, source_target_pairs={{1,0},{2,3},{5,4},{6,7},{9,8},{10,11},{13,12},{14,15},{17,16},{18,... | collective-permute-start | bytes 3145736 | tf_op jit(solution)/shard_map/ppermute | solution.py:669
  399.0 22.2 %collective-permute-start.56 = (bf16[2,256,512]{2,1,0:T(8,128)(2,1)S(1)}, bf16[2,256,512]{2,1,0:T(8,128)(2,1)S(1)}, u32[]{:S(2)}, u32[]{:S(2)}) collective-permute-start(bf16[2,256,512]{2,1,0:T(8,128)(2,1)S(1)} %get-tuple-element.229), channel_id=1, source_target_pairs={{0,8},{4,12},{8,0},{12,4},{16,24},{20,28},{24,16},{28,20},{1,9},{5... | collective-permute-start | bytes 1572872 | tf_op jit(solution)/shard_map/ppermute | solution.py:20
  408.8 14.9 %collective-permute-start.57 = (bf16[2,256,512]{2,1,0:T(8,128)(2,1)S(1)}, bf16[2,256,512]{2,1,0:T(8,128)(2,1)S(1)}, u32[]{:S(2)}, u32[]{:S(2)}) collective-permute-start(bf16[2,256,512]{2,1,0:T(8,128)(2,1)S(1)} %get-tuple-element.230), channel_id=1, source_target_pairs={{0,16},{4,20},{8,24},{12,28},{16,0},{20,4},{24,8},{28,12},{1,17},{... | collective-permute-start | bytes 1572872 | tf_op jit(solution)/shard_map/ppermute | solution.py:20
  410.1 19.3 %collective-permute-start.53 = (bf16[128,1536]{1,0:T(8,128)(2,1)S(1)}, bf16[128,1536]{1,0:T(8,128)(2,1)S(1)}, u32[]{:S(2)}, u32[]{:S(2)}) collective-permute-start(bf16[128,1536]{1,0:T(8,128)(2,1)S(1)} %fusion.20), channel_id=1, source_target_pairs={{0,16},{4,20},{8,24},{12,28},{16,0},{20,4},{24,8},{28,12},{1,17},{... | collective-permute-start | bytes 1179656 | tf_op jit(solution)/shard_map/ppermute | solution.py:20
  412.0 17.4 %collective-permute-start.54 = (bf16[128,1536]{1,0:T(8,128)(2,1)S(1)}, bf16[128,1536]{1,0:T(8,128)(2,1)S(1)}, u32[]{:S(2)}, u32[]{:S(2)}) collective-permute-start(bf16[128,1536]{1,0:T(8,128)(2,1)S(1)} %fusion.21), channel_id=1, source_target_pairs={{0,8},{4,12},{8,0},{12,4},{16,24},{20,28},{24,16},{28,20},{1,9},{5... | collective-permute-start | bytes 1179656 | tf_op jit(solution)/shard_map/ppermute | solution.py:20
  421.2 19.8 %collective-permute-start.59 = (bf16[128,5120]{1,0:T(8,128)(2,1)S(1)}, bf16[128,5120]{1,0:T(8,128)(2,1)S(1)}, u32[]{:S(2)}, u32[]{:S(2)}) collective-permute-start(bf16[128,5120]{1,0:T(8,128)(2,1)S(1)} %add_convert_fusion.1), channel_id=1, source_target_pairs={{1,2},{2,1},{5,6},{6,5},{9,10},{10,9},{13,14},{14,13},{17,18},{18,... | collective-permute-start | bytes 3932168 | tf_op jit(solution)/shard_map/ppermute | solution.py:669
  429.8 11.2 %collective-permute-start.58 = (bf16[64,3072]{1,0:T(8,128)(2,1)S(1)}, bf16[64,3072]{1,0:T(8,128)(2,1)S(1)}, u32[]{:S(2)}, u32[]{:S(2)}) collective-permute-start(bf16[64,3072]{1,0:T(8,128)(2,1)S(1)} %fusion.23), channel_id=1, source_target_pairs={{0,1},{1,0},{2,3},{3,2},{4,5},{5,4},{6,7},{7,6},{8,9},{9,8},{10,11... | collective-permute-start | bytes 1179656 | tf_op jit(solution)/shard_map/ppermute | solution.py:25
  432.4 8.5 %collective-permute-start.60 = (bf16[256,512]{1,0:T(8,128)(2,1)S(1)}, bf16[256,512]{1,0:T(8,128)(2,1)S(1)}, u32[]{:S(2)}, u32[]{:S(2)}) collective-permute-start(bf16[256,512]{1,0:T(8,128)(2,1)S(1)} %fusion.24), channel_id=1, source_target_pairs={{0,16},{4,20},{8,24},{12,28},{16,0},{20,4},{24,8},{28,12},{1,17},{... | collective-permute-start | bytes 786440 | tf_op jit(solution)/shard_map/ppermute | solution.py:20
  446.4 19.2 %collective-permute-start.64 = (bf16[160,1024]{1,0:T(8,128)(2,1)S(1)}, bf16[160,1024]{1,0:T(8,128)(2,1)S(1)}, u32[]{:S(2)}, u32[]{:S(2)}) collective-permute-start(bf16[160,1024]{1,0:T(8,128)(2,1)S(1)} %constant_dynamic-slice_fusion.1), channel_id=1, source_target_pairs={{0,1},{1,0},{2,3},{3,2},{4,5},{5,4},{6,7},{7,6},{8,9},{9,8},{10,11... | collective-permute-start | bytes 983048 | tf_op jit(solution)/shard_map/ppermute | solution.py:25
  453.5 36.4 %collective-permute-start.65 = (bf16[128,5120]{1,0:T(8,128)(2,1)S(1)}, bf16[128,5120]{1,0:T(8,128)(2,1)S(1)}, u32[]{:S(2)}, u32[]{:S(2)}) collective-permute-start(bf16[128,5120]{1,0:T(8,128)(2,1)S(1)} %add_convert_fusion), channel_id=1, source_target_pairs={{1,0},{2,3},{5,4},{6,7},{9,8},{10,11},{13,12},{14,15},{17,16},{18,... | collective-permute-start | bytes 3932168 | tf_op jit(solution)/shard_map/ppermute | solution.py:669
  455.0 9.8 %collective-permute-start.63 = (bf16[32,3072]{1,0:T(8,128)(2,1)S(1)}, bf16[32,3072]{1,0:T(8,128)(2,1)S(1)}, u32[]{:S(2)}, u32[]{:S(2)}) collective-permute-start(bf16[32,3072]{1,0:T(8,128)(2,1)S(1)} %constant_dynamic-slice_fusion.2), channel_id=1, source_target_pairs={{0,2},{1,3},{2,0},{3,1},{4,6},{5,7},{6,4},{7,5},{8,10},{9,11},{10,... | collective-permute-start | bytes 589832 | tf_op jit(solution)/shard_map/ppermute | solution.py:25
  489.9 12.0 %collective-permute-start.66 = (bf16[32,3072]{1,0:T(8,128)(2,1)S(1)}, bf16[32,3072]{1,0:T(8,128)(2,1)S(1)}, u32[]{:S(2)}, u32[]{:S(2)}) collective-permute-start(bf16[32,3072]{1,0:T(8,128)(2,1)S(1)} %add_convert_fusion.17), channel_id=1, source_target_pairs={{0,2},{1,3},{2,0},{3,1},{4,6},{5,7},{6,4},{7,5},{8,10},{9,11},{10,... | collective-permute-start | bytes 589832 | tf_op jit(solution)/shard_map/ppermute | solution.py:25
  490.1 11.8 %collective-permute-start.67 = (bf16[80,1024]{1,0:T(8,128)(2,1)S(1)}, bf16[80,1024]{1,0:T(8,128)(2,1)S(1)}, u32[]{:S(2)}, u32[]{:S(2)}) collective-permute-start(bf16[80,1024]{1,0:T(8,128)(2,1)S(1)} %constant_dynamic-slice_fusion), channel_id=1, source_target_pairs={{0,2},{1,3},{2,0},{3,1},{4,6},{5,7},{6,4},{7,5},{8,10},{9,11},{10,... | collective-permute-start | bytes 491528 | tf_op jit(solution)/shard_map/ppermute | solution.py:25
  502.0 11.8 %collective-permute-start.68 = (bf16[64,3072]{1,0:T(8,128)(2,1)S(1)}, bf16[64,3072]{1,0:T(8,128)(2,1)S(1)}, u32[]{:S(2)}, u32[]{:S(2)}) collective-permute-start(bf16[64,3072]{1,0:T(8,128)(2,1)S(1)} %pad_maximum_fusion.4), channel_id=1, source_target_pairs={{0,1},{1,0},{2,3},{3,2},{4,5},{5,4},{6,7},{7,6},{8,9},{9,8},{10,11... | collective-permute-start | bytes 1179656 | tf_op jit(solution)/shard_map/ppermute | solution.py:25
  502.5 10.1 %collective-permute-start.69 = (bf16[80,1024]{1,0:T(8,128)(2,1)S(1)}, bf16[80,1024]{1,0:T(8,128)(2,1)S(1)}, u32[]{:S(2)}, u32[]{:S(2)}) collective-permute-start(bf16[80,1024]{1,0:T(8,128)(2,1)S(1)} %add_convert_fusion.18), channel_id=1, source_target_pairs={{0,2},{1,3},{2,0},{3,1},{4,6},{5,7},{6,4},{7,5},{8,10},{9,11},{10,... | collective-permute-start | bytes 491528 | tf_op jit(solution)/shard_map/ppermute | solution.py:25
  (145 other events, 1036.3 us)
where the time goes:
time: 532 us; the launch traced here: 525 us
  waiting for transfers between devices  147 us (28%)
  Pallas kernels  140 us (26%)
  starting transfers between devices  115 us (22%)
  local copies, waits for them, and re-layouts  48.7 us (9%)
  matrix products  34.6 us (7%)
  other arithmetic  33.1 us (6%)
  between operations  6.14 us (1%)
    ppermute x47, waiting for transfers between devices, flip(): return lax.ppermute(value, 'dp', [(i, i ^ bit) for i in range(n)])  56.6 us
    ppermute x18, waiting for transfers between devices, rep_flip(): return lax.ppermute(value, 'rep', [(i, i ^ bit) for i in range(n)])  53.7 us
    ppermute x47, starting transfers between devices, flip(): return lax.ppermute(value, 'dp', [(i, i ^ bit) for i in range(n)])  46.9 us
    pallas_call x9, Pallas kernels, gradient_blocks(): pl.pallas_call(body, out_shape=out_shape, grid_spec=pltpu.PrefetchScalarG...  40.8 us
    ppermute x18, starting transfers between devices, rep_flip(): return lax.ppermute(value, 'rep', [(i, i ^ bit) for i in range(n)])  40.5 us
    unnamed x277, local copies, waits for them, and re-layouts  37.5 us
    ppermute x6, waiting for transfers between devices, along(): return lax.ppermute(self.value, 'rep', pairs)  33 us
    dot_general x7, matrix products, matmul(): return jnp.dot(left, right, preferred_element_type=F32)  25.5 us
  transfers between devices with their start and end apart: 75, of which 36 were waited for; matrix products, arithmetic and copies ran while one was open for 13% of the time, Pallas kernels for 25%

commit v1 on v0

--- a/solution.py
+++ b/solution.py
@@ -1056,9 +1056,10 @@
     )
     lengths = [v.shape[0] for v in vectors]
     summed = jnp.concatenate(vectors).reshape(-1, 128)
-    for bit in range(bits - 1):
+    summed = summed + flip(summed, 1)
+    up_flying, token, summed = together(up_flying, red_skip.token, summed)
+    for bit in range(1, bits - 1):
         summed = summed + flip(summed, 1 << bit)
-    up_flying, token = together(up_flying, red_skip.token)
     red_up.landed(up_flying)
     red_up.rows()
     up_line = red_up.along()
@@ -1073,7 +1074,7 @@
     line = red_down.along()
     result = mixed + matmul(active, full_down) + (c_down + token[0, 0])
     output = (result * keep_rows).astype(BF16)
-    grad_joined = matmul_nt(base_low, full_skip).astype(BF16)
+    grad_joined = (matmul_nt(base_low, full_skip) + token[0, 0]).astype(BF16)
     flying, up_line, grad_joined, summed = together(flying, up_line, grad_joined, summed)
     red_mid.near_landed(flying)
     red_up.along_landed(up_line)

time: 532 us -> 531 us (level)
  starting transfers between devices: 115 us -> 105 us
  waiting for transfers between devices: 147 us -> 155 us
    ppermute x18, waiting for transfers between devices: 53.7 us -> 61 us  [rep_flip(): return lax.ppermute(value, 'rep', [(i, i ^ bit) for i in range(n)])]
    ppermute x18, starting transfers between devices: 40.5 us -> 34.7 us  [rep_flip(): return lax.ppermute(value, 'rep', [(i, i ^ bit) for i in range(n)])]
  transfers between devices with their start and end apart: 75 -> 75, of which waited for: 36 -> 38; matrix products, arithmetic and copies ran while one was open for 13% -> 13% of each run, Pallas kernels for 25% -> 25%
where the time goes in v1:
time: 531 us; the launch traced here: 524 us
  waiting for transfers between devices  155 us (29%)
  Pallas kernels  140 us (26%)
  starting transfers between devices  105 us (20%)
  local copies, waits for them, and re-layouts  49.3 us (9%)
  matrix products  35.5 us (7%)
  other arithmetic  33.1 us (6%)
  between operations  6.11 us (1%)
    ppermute x18, waiting for transfers between devices, rep_flip(): return lax.ppermute(value, 'rep', [(i, i ^ bit) for i in range(n)])  61 us
    ppermute x47, waiting for transfers between devices, flip(): return lax.ppermute(value, 'dp', [(i, i ^ bit) for i in range(n)])  59.6 us
    ppermute x47, starting transfers between devices, flip(): return lax.ppermute(value, 'dp', [(i, i ^ bit) for i in range(n)])  42.9 us
    pallas_call x9, Pallas kernels, gradient_blocks(): pl.pallas_call(body, out_shape=out_shape, grid_spec=pltpu.PrefetchScalarG...  40.8 us
    unnamed x277, local copies, waits for them, and re-layouts  38.1 us
    ppermute x18, starting transfers between devices, rep_flip(): return lax.ppermute(value, 'rep', [(i, i ^ bit) for i in range(n)])  34.7 us
    ppermute x6, waiting for transfers between devices, along(): return lax.ppermute(self.value, 'rep', pairs)  30.6 us
    dot_general x7, matrix products, matmul(): return jnp.dot(left, right, preferred_element_type=F32)  25.6 us
  transfers between devices with their start and end apart: 75, of which 38 were waited for; matrix products, arithmetic and copies ran while one was open for 13% of the time, Pallas kernels for 25%

profile of v1, /device:TPU:0, one launch (start us, length us, event | category | flops | bytes accessed | tf_op | source)
XLA Modules:
  0.0 524.0 jit_solution(8570237111946689204)
XLA Ops:
  7.2 3.7 collective-permute-start
  14.4 3.4 collective-permute-done.refs_1_.refs_2_.refs_0_
  20.3 3.4 collective-permute-start.5
  27.4 4.0 collective-permute-done.1.refs_1_
  31.4 4.2 collective-permute-done.5.refs_3_.refs_1_.refs_0_
  61.6 2.4 assemble.5
  64.1 2.4 add_reduce_fusion
  69.2 3.9 all-to-all-start
  73.0 2.3 collective-permute-done.14.refs_5_.refs_1_.refs_0_
  77.1 2.2 pack.22
  86.4 13.8 %collective-permute-done.18.refs_5_.refs_1_.refs_0_ = bf16[128,1024]{1,0:T(8,128)(2,1)S(1)} collective-permute-done((bf16[128,1024]{1,0:T(8,128)(2,1)S(1)}, bf16[128,1024]{1,0:T(8,128)(2,1)S(1)}, u32[]{:S(2)}, u32[]{:S(2)}) %collective-permute-start.18) | collective-permute-done | bytes 262176 | tf_op jit(solution)/shard_map/ppermute | solution.py:25
  101.9 2.3 collective-permute-done.15.refs_1_
  112.6 2.5 collective-permute-start.24
  118.8 4.6 assemble.6
  123.5 3.7 convolution_convert_fusion
  132.0 16.6 %attend.1.refs_4_ = bf16[8,2,32,1024]{3,2,1,0:T(8,128)(2,1)S(1)} custom-call(f32[16]{0:T(128)S(1)} %multiply_power_fusion.slope_ref, bf16[8,2,32,3072]{3,2,1,0:T(8,128)(2,1)S(1)} %bitcast.134, bf16[8,2,32,3072]{3,2,1,0:T(8,128)(2,1)S(1)} %bitcast.135, bf16[8,2,32,3072]{3,2,1,0:T(8,128)(2,1)S(1)} %bitcast.136, f32[2,256,256]{2,1,0:T(8,128)S(1)} %copy-done.83, ...), custom_call_target="tpu_custom_call" | custom-call | flops 9200000000 | bytes 1024 | tf_op jit(solution)/shard_map/attend/pallas_call | solution.py:511
  151.5 4.5 all-to-all-start.1
  167.7 5.2 assemble.8
  172.9 3.2 copy-done.8
  177.2 2.1 convolution_convert_fusion.2.refs_0_.refs_1_
  186.0 2.2 collective-permute-start.30
  189.3 9.0 %fusion.4 = (bf16[512,4096]{1,0:T(8,128)(2,1)}, bf16[512,4096]{1,0:T(8,128)(2,1)S(1)}) fusion(f32[4096]{0:T(1024)S(1)} %broadcast_add_fusion, bf16[512,1024]{1,0:T(8,128)(2,1)S(1)} %add_convert_fusion.5.refs_0_, bf16[1024,4096]{1,0:T(8,128)(2,1)S(1)} %bitcast.143), kind=kOutput, calls=%fused_computation.5 | convolution fusion | flops 4320133120 | bytes 17842176 | tf_op jit(solution)/shard_map/dot_general | solution.py:835
  198.9 2.6 collective-permute-start.31
  203.6 4.6 gradient.9
  209.9 8.6 %collective-permute-done.32.refs_1_ = bf16[3072,512]{1,0:T(8,128)(2,1)S(1)} collective-permute-done((bf16[3072,512]{1,0:T(8,128)(2,1)S(1)}, bf16[3072,512]{1,0:T(8,128)(2,1)S(1)}, u32[]{:S(2)}, u32[]{:S(2)}) %collective-permute-start.32) | collective-permute-done | bytes 3145760 | tf_op jit(solution)/shard_map/ppermute | solution.py:20
  218.6 2.5 assemble.9
  221.2 6.7 %hidden_gradient.1 = (bf16[512,4096]{1,0:T(8,128)(2,1)S(1)}, f32[1,4096]{1,0:T(1,128)S(1)}) custom-call(bf16[512,1024]{1,0:T(8,128)(2,1)S(1)} %bitcast_multiply_fusion.grad_ref.result_ref, bf16[4096,1024]{1,0:T(8,128)(2,1)S(1)} %get-tuple-element.175.w_ref, bf16[512,4096]{1,0:T(8,128)(2,1)S(1)} %copy-done.23), custom_call_target="tpu_custom_call" | custom-call | flops 3449999872 | bytes 1024 | tf_op jit(solution)/shard_map/hidden_gradient/pallas_call | solution.py:736
  227.9 6.5 %gradient.10 = (bf16[4,128,4096]{2,1,0:T(8,128)(2,1)}, f32[8,128]{1,0:T(8,128)}) custom-call(s32[1]{0:T(128)} %bitcast.6.d_ref, bf16[512,1024]{1,0:T(8,128)(2,1)S(1)} %add_convert_fusion.5.refs_0_, bf16[1,512,4096]{2,1,0:T(8,128)(2,1)S(1)} %bitcast.140), custom_call_target="tpu_custom_call" | custom-call | flops 2875000064 | bytes 1024 | tf_op jit(solution)/shard_map/gradient/pallas_call | solution.py:452
  234.6 5.3 %gradient.11 = (bf16[2,512,512]{2,1,0:T(8,128)(2,1)}, bf16[2,512,512]{2,1,0:T(8,128)(2,1)S(1)}, bf16[2,512,512]{2,1,0:T(8,128)(2,1)}, bf16[2,512,512]{2,1,0:T(8,128)(2,1)S(1)}, f32[8,128]{1,0:T(8,128)S(1)}) custom-call(s32[1]{0:T(128)} %bitcast.6.d_ref, bf16[512,4096]{1,0:T(8,128)(2,1)S(1)} %get-tuple-element.293.refs_0_, ...), custom_call_target="tpu_custom_call" | custom-call | flops 2875000064 | bytes 1024 | tf_op jit(solution)/shard_map/gradient/pallas_call | solution.py:452
  244.6 11.4 %mixed_gradient.1 = (f32[512,1024]{1,0:T(8,128)S(1)}, bf16[512,1024]{1,0:T(8,128)(2,1)S(1)}, bf16[512,1024]{1,0:T(8,128)(2,1)S(1)}, f32[8,1024]{1,0:T(8,128)S(1)}) custom-call(bf16[512,4096]{1,0:T(8,128)(2,1)} %copy-done.6, bf16[1024,4096]{1,0:T(8,128)(2,1)} %copy-done.8, bf16[1024,1024]{1,0:T(8,128)(2,1)S(1)} %copy-done.43, ...), custom_call_target="tpu_custom_call" | custom-call | flops 2300000000 | bytes 1024 | tf_op jit(solution)/shard_map/mixed_gradient/pallas_call | solution.py:787
  258.2 9.3 %collective-permute-done.34 = bf16[2,512,512]{2,1,0:T(8,128)(2,1)S(1)} collective-permute-done((bf16[2,512,512]{2,1,0:T(8,128)(2,1)}, bf16[2,512,512]{2,1,0:T(8,128)(2,1)S(1)}, u32[]{:S(2)}, u32[]{:S(2)}) %collective-permute-start.34) | collective-permute-done | bytes 1048608 | tf_op jit(solution)/shard_map/ppermute | solution.py:20
  274.4 4.2 all-to-all-start.2
  278.6 2.2 copy-done.7
  282.0 10.4 %gradient.13 = (bf16[2,128,2560]{2,1,0:T(8,128)(2,1)}, bf16[2,128,2560]{2,1,0:T(8,128)(2,1)S(1)}, bf16[2,128,2560]{2,1,0:T(8,128)(2,1)}, bf16[2,128,2560]{2,1,0:T(8,128)(2,1)S(1)}, f32[8,128]{1,0:T(8,128)S(1)}) custom-call(s32[1]{0:T(128)} %bitcast.6.d_ref, bf16[512,1024]{1,0:T(8,128)(2,1)S(1)} %add_convert_fusion.5.refs_0_, ...), custom_call_target="tpu_custom_call" | custom-call | flops 2875000064 | bytes 1024 | tf_op jit(solution)/shard_map/gradient/pallas_call | solution.py:452
  299.6 4.0 collective-permute-start.42
  304.7 20.4 %attend_back.1 = (bf16[3,8,2,32,1024]{4,3,2,1,0:T(8,128)(2,1)S(1)}, f32[8,128]{1,0:T(8,128)S(1)}) custom-call(f32[16]{0:T(128)S(1)} %multiply_power_fusion.slope_ref, bf16[8,2,32,3072]{3,2,1,0:T(8,128)(2,1)S(1)} %bitcast.137, bf16[8,2,32,3072]{3,2,1,0:T(8,128)(2,1)S(1)} %bitcast.138, bf16[8,2,32,3072]{3,2,1,0:T(8,128)(2,1)S(1)} %bitcast.139, ...), custom_call_target="tpu_custom_call" | custom-call | flops 2300000000 | bytes 1024 | tf_op jit(solution)/shard_map/attend_back/pallas_call | solution.py:573
  325.1 3.9 copy-done.17
  329.0 4.7 normed_gradient.1.refs_2_
  333.7 4.4 all-to-all-start.3
  338.4 2.6 add_convert_fusion.4
  344.5 3.5 gradient.14
  349.6 3.9 all-to-all-done.3
  353.6 3.3 multiply_reduce_fusion
  365.5 3.0 collective-permute-done.47
  368.6 3.3 collective-permute-done.45
  371.9 3.3 collective-permute-done.46
  381.3 4.2 gradient.16
  396.0 4.5 add_convert_fusion
  400.5 7.4 %collective-permute-done.52 = bf16[128,5120]{1,0:T(8,128)(2,1)S(1)} collective-permute-done((bf16[128,5120]{1,0:T(8,128)(2,1)S(1)}, bf16[128,5120]{1,0:T(8,128)(2,1)S(1)}, u32[]{:S(2)}, u32[]{:S(2)}) %collective-permute-start.52) | collective-permute-done | bytes 1310752 | tf_op jit(solution)/shard_map/ppermute | solution.py:669
  411.2 8.6 %collective-permute-done.56 = bf16[2,256,512]{2,1,0:T(8,128)(2,1)S(1)} collective-permute-done((bf16[2,256,512]{2,1,0:T(8,128)(2,1)S(1)}, bf16[2,256,512]{2,1,0:T(8,128)(2,1)S(1)}, u32[]{:S(2)}, u32[]{:S(2)}) %collective-permute-start.56) | collective-permute-done | bytes 524320 | tf_op jit(solution)/shard_map/ppermute | solution.py:20
  420.6 2.2 collective-permute-done.57
  422.8 5.7 %collective-permute-done.53 = bf16[128,1536]{1,0:T(8,128)(2,1)S(1)} collective-permute-done((bf16[128,1536]{1,0:T(8,128)(2,1)S(1)}, bf16[128,1536]{1,0:T(8,128)(2,1)S(1)}, u32[]{:S(2)}, u32[]{:S(2)}) %collective-permute-start.53) | collective-permute-done | bytes 393248 | tf_op jit(solution)/shard_map/ppermute | solution.py:20
  428.9 2.5 collective-permute-start.58
  434.0 5.5 %multiply_convert_fusion.1 = bf16[512,1024]{1,0:T(8,128)(2,1)} fusion(f32[512,1024]{1,0:T(8,128)S(1)} %copy-done.5, bf16[512,4096]{1,0:T(8,128)(2,1)S(1)} %copy-done.26, bf16[4096,1024]{1,0:T(8,128)(2,1)S(1)} %bitcast.145, f32[512]{0:T(512)S(1)} %slice_reduce_fusion, f32[1024]{0:T(1024)S(1)} %broadcast_add_fusion.1), kind=kOutput, calls=%fused_computation.14 | convolution fusion | flops 4297064448 | bytes 15734784 | tf_op jit(solution)/shard_map/dot_general | solution.py:835
  445.2 6.0 %collective-permute-start.64 = (bf16[160,1024]{1,0:T(8,128)(2,1)S(1)}, bf16[160,1024]{1,0:T(8,128)(2,1)S(1)}, u32[]{:S(2)}, u32[]{:S(2)}) collective-permute-start(bf16[160,1024]{1,0:T(8,128)(2,1)S(1)} %constant_dynamic-slice_fusion.1), channel_id=1, source_target_pairs={{0,1},{1,0},{2,3},{3,2},{4,5},{5,4},{6,7},{7,6},{8,9},{9,8},{10,11... | collective-permute-start | bytes 983048 | tf_op jit(solution)/shard_map/ppermute | solution.py:25
  453.0 3.2 collective-permute-start.63
  457.7 4.4 collective-permute-done.63
  462.5 23.1 %collective-permute-done.65 = bf16[128,5120]{1,0:T(8,128)(2,1)S(1)} collective-permute-done((bf16[128,5120]{1,0:T(8,128)(2,1)S(1)}, bf16[128,5120]{1,0:T(8,128)(2,1)S(1)}, u32[]{:S(2)}, u32[]{:S(2)}) %collective-permute-start.65) | collective-permute-done | bytes 1310752 | tf_op jit(solution)/shard_map/ppermute | solution.py:669
  486.0 2.9 collective-permute-start.67
  490.3 9.1 %collective-permute-done.67 = bf16[80,1024]{1,0:T(8,128)(2,1)S(1)} collective-permute-done((bf16[80,1024]{1,0:T(8,128)(2,1)S(1)}, bf16[80,1024]{1,0:T(8,128)(2,1)S(1)}, u32[]{:S(2)}, u32[]{:S(2)}) %collective-permute-start.67) | collective-permute-done | bytes 163872 | tf_op jit(solution)/shard_map/ppermute | solution.py:25
  499.6 2.2 collective-permute-start.69
  504.3 6.0 %collective-permute-done.69 = bf16[80,1024]{1,0:T(8,128)(2,1)S(1)} collective-permute-done((bf16[80,1024]{1,0:T(8,128)(2,1)S(1)}, bf16[80,1024]{1,0:T(8,128)(2,1)S(1)}, u32[]{:S(2)}, u32[]{:S(2)}) %collective-permute-start.69) | collective-permute-done | bytes 163872 | tf_op jit(solution)/shard_map/ppermute | solution.py:25
  510.3 2.2 collective-permute-done.68
  514.2 6.9 %collective-permute-done.70 = bf16[160,1024]{1,0:T(8,128)(2,1)S(1)} collective-permute-done((bf16[160,1024]{1,0:T(8,128)(2,1)S(1)}, bf16[160,1024]{1,0:T(8,128)(2,1)S(1)}, u32[]{:S(2)}, u32[]{:S(2)}) %collective-permute-start.70) | collective-permute-done | bytes 327712 | tf_op jit(solution)/shard_map/ppermute | solution.py:25
  (512 shorter events, 175.0 us)
Async XLA Ops:
  7.2 10.6 %collective-permute-start = (bf16[64,1024]{1,0:T(8,128)(2,1)S(1)}, bf16[64,1024]{1,0:T(8,128)(2,1)S(1)}, u32[]{:S(2)}, u32[]{:S(2)}) collective-permute-start(bf16[64,1024]{1,0:T(8,128)(2,1)S(1)} %own_chunk.4.refs_0_), channel_id=1, source_target_pairs={{0,2},{1,3},{2,0},{3,1},{4,6},{5,7},{6,4},{7,5},{8,10},{9,11},{10,... | collective-permute-start | bytes 393224 | tf_op jit(solution)/shard_map/ppermute | solution.py:25
  10.9 12.8 %collective-permute-start.3 = (s32[2,129]{1,0:T(2,128)S(1)}, s32[2,129]{1,0:T(2,128)S(1)}, u32[]{:S(2)}, u32[]{:S(2)}) collective-permute-start(s32[2,129]{1,0:T(2,128)S(1)} %pad_add_fusion.2), channel_id=1, source_target_pairs={{0,8},{4,12},{8,0},{12,4},{16,24},{20,28},{24,16},{28,20},{1,9},{5... | collective-permute-start | bytes 3104 | tf_op jit(solution)/shard_map/ppermute | solution.py:20
  18.7 12.7 %collective-permute-start.1 = (bf16[128,1024]{1,0:T(8,128)(2,1)S(1)}, bf16[128,1024]{1,0:T(8,128)(2,1)S(1)}, u32[]{:S(2)}, u32[]{:S(2)}) collective-permute-start(bf16[128,1024]{1,0:T(8,128)(2,1)S(1)} %get-tuple-element.136), channel_id=1, source_target_pairs={{0,1},{1,0},{2,3},{3,2},{4,5},{5,4},{6,7},{7,6},{8,9},{9,8},{10,11... | collective-permute-start | bytes 786440 | tf_op jit(solution)/shard_map/ppermute | solution.py:25
  20.3 15.4 %collective-permute-start.5 = (bf16[128,1024]{1,0:T(8,128)(2,1)S(1)}, bf16[128,1024]{1,0:T(8,128)(2,1)S(1)}, u32[]{:S(2)}, u32[]{:S(2)}) collective-permute-start(bf16[128,1024]{1,0:T(8,128)(2,1)S(1)} %own_chunk.5.refs_0_), channel_id=1, source_target_pairs={{0,2},{1,3},{2,0},{3,1},{4,6},{5,7},{6,4},{7,5},{8,10},{9,11},{10,... | collective-permute-start | bytes 786440 | tf_op jit(solution)/shard_map/ppermute | solution.py:25
  40.3 12.8 %collective-permute-start.10 = (bf16[256,1024]{1,0:T(8,128)(2,1)}, bf16[256,1024]{1,0:T(8,128)(2,1)S(1)}, u32[]{:S(2)}, u32[]{:S(2)}) collective-permute-start(bf16[256,1024]{1,0:T(8,128)(2,1)} %get-tuple-element.143), channel_id=1, source_target_pairs={{0,1},{1,0},{2,3},{3,2},{4,5},{5,4},{6,7},{7,6},{8,9},{9,8},{10,11... | collective-permute-start | bytes 1572872 | tf_op jit(solution)/shard_map/ppermute | solution.py:25
  45.4 9.2 %collective-permute-start.8 = (bf16[384,512]{1,0:T(8,128)(2,1)S(1)}, bf16[384,512]{1,0:T(8,128)(2,1)}, u32[]{:S(2)}, u32[]{:S(2)}) collective-permute-start(bf16[384,512]{1,0:T(8,128)(2,1)S(1)} %get-tuple-element.140.refs_0_), channel_id=1, source_target_pairs={{0,16},{4,20},{8,24},{12,28},{16,0},{20,4},{24,8},{28,12},{1,17},{... | collective-permute-start | bytes 1179656 | tf_op jit(solution)/shard_map/ppermute | solution.py:20
  47.0 9.1 %collective-permute-start.9 = (bf16[384,512]{1,0:T(8,128)(2,1)}, bf16[384,512]{1,0:T(8,128)(2,1)}, u32[]{:S(2)}, u32[]{:S(2)}) collective-permute-start(bf16[384,512]{1,0:T(8,128)(2,1)} %get-tuple-element.141.refs_2_), channel_id=1, source_target_pairs={{0,8},{4,12},{8,0},{12,4},{16,24},{20,28},{24,16},{28,20},{1,9},{5... | collective-permute-start | bytes 1179656 | tf_op jit(solution)/shard_map/ppermute | solution.py:20
  59.0 16.3 %collective-permute-start.12 = (bf16[384,512]{1,0:T(8,128)(2,1)S(1)}, bf16[384,512]{1,0:T(8,128)(2,1)S(1)}, u32[]{:S(2)}, u32[]{:S(2)}) collective-permute-start(bf16[384,512]{1,0:T(8,128)(2,1)S(1)} %get-tuple-element.145.refs_2_.refs_1_.refs_0_), channel_id=1, source_target_pairs={{0,8},{4,12},{8,0},{12,4},{16,24},{20,28},{24,16},{28,20},{1,9},{5... | collective-permute-start | bytes 1179656 | tf_op jit(solution)/shard_map/ppermute | solution.py:20
  59.6 16.5 %collective-permute-start.13 = (bf16[384,512]{1,0:T(8,128)(2,1)S(1)}, bf16[384,512]{1,0:T(8,128)(2,1)}, u32[]{:S(2)}, u32[]{:S(2)}) collective-permute-start(bf16[384,512]{1,0:T(8,128)(2,1)S(1)} %get-tuple-element.147.refs_2_), channel_id=1, source_target_pairs={{0,16},{4,20},{8,24},{12,28},{16,0},{20,4},{24,8},{28,12},{1,17},{... | collective-permute-start | bytes 1179656 | tf_op jit(solution)/shard_map/ppermute | solution.py:20
  60.8 14.5 %collective-permute-start.14 = (bf16[128,1024]{1,0:T(8,128)(2,1)S(1)}, bf16[128,1024]{1,0:T(8,128)(2,1)S(1)}, u32[]{:S(2)}, u32[]{:S(2)}) collective-permute-start(bf16[128,1024]{1,0:T(8,128)(2,1)S(1)} %own_chunk.6.refs_0_), channel_id=1, source_target_pairs={{0,2},{1,3},{2,0},{3,1},{4,6},{5,7},{6,4},{7,5},{8,10},{9,11},{10,... | collective-permute-start | bytes 786440 | tf_op jit(solution)/shard_map/ppermute | solution.py:25
  69.2 36.9 %all-to-all-start = ((bf16[8,64,1024]{2,1,0:T(8,128)(2,1)}), bf16[8,64,1024]{2,1,0:T(8,128)(2,1)S(1)}, u32[]{:S(2)}, u32[]{:S(2)}) async-start(bf16[8,64,1024]{2,1,0:T(8,128)(2,1)} %bitcast.10), calls=%async_computation | async-start | bytes 2097152 | tf_op jit(solution)/shard_map/all_to_all | solution.py:947
  79.3 25.0 %collective-permute-start.15 = (bf16[768,512]{1,0:T(8,128)(2,1)S(1)}, bf16[768,512]{1,0:T(8,128)(2,1)S(1)}, u32[]{:S(2)}, u32[]{:S(2)}) collective-permute-start(bf16[768,512]{1,0:T(8,128)(2,1)S(1)} %get-tuple-element.148.refs_0_), channel_id=1, source_target_pairs={{0,16},{4,20},{8,24},{12,28},{16,0},{20,4},{24,8},{28,12},{1,17},{... | collective-permute-start | bytes 2359304 | tf_op jit(solution)/shard_map/ppermute | solution.py:20
  80.8 24.3 %collective-permute-start.16 = (bf16[768,512]{1,0:T(8,128)(2,1)S(1)}, bf16[768,512]{1,0:T(8,128)(2,1)S(1)}, u32[]{:S(2)}, u32[]{:S(2)}) collective-permute-start(bf16[768,512]{1,0:T(8,128)(2,1)S(1)} %get-tuple-element.149.refs_2_), channel_id=1, source_target_pairs={{0,8},{4,12},{8,0},{12,4},{16,24},{20,28},{24,16},{28,20},{1,9},{5... | collective-permute-start | bytes 2359304 | tf_op jit(solution)/shard_map/ppermute | solution.py:20
  83.0 19.0 %collective-permute-start.17 = (bf16[256,1024]{1,0:T(8,128)(2,1)S(1)}, bf16[256,1024]{1,0:T(8,128)(2,1)S(1)}, u32[]{:S(2)}, u32[]{:S(2)}) collective-permute-start(bf16[256,1024]{1,0:T(8,128)(2,1)S(1)} %get-tuple-element.150), channel_id=1, source_target_pairs={{0,1},{1,0},{2,3},{3,2},{4,5},{5,4},{6,7},{7,6},{8,9},{9,8},{10,11... | collective-permute-start | bytes 1572872 | tf_op jit(solution)/shard_map/ppermute | solution.py:25
  84.3 16.0 %collective-permute-start.18 = (bf16[128,1024]{1,0:T(8,128)(2,1)S(1)}, bf16[128,1024]{1,0:T(8,128)(2,1)S(1)}, u32[]{:S(2)}, u32[]{:S(2)}) collective-permute-start(bf16[128,1024]{1,0:T(8,128)(2,1)S(1)} %own_chunk.7.refs_0_), channel_id=1, source_target_pairs={{0,2},{1,3},{2,0},{3,1},{4,6},{5,7},{6,4},{7,5},{8,10},{9,11},{10,... | collective-permute-start | bytes 786440 | tf_op jit(solution)/shard_map/ppermute | solution.py:25
  110.7 8.1 %collective-permute-start.19 = (bf16[3072,512]{1,0:T(8,128)(2,1)S(1)}, bf16[3072,512]{1,0:T(8,128)(2,1)S(1)}, u32[]{:S(2)}, u32[]{:S(2)}) collective-permute-start(bf16[3072,512]{1,0:T(8,128)(2,1)S(1)} %get-tuple-element.151.refs_0_.refs_2_), channel_id=1, source_target_pairs={{0,4},{4,0},{8,12},{12,8},{16,20},{20,16},{24,28},{28,24},{1,5},{5... | collective-permute-start | bytes 9437192 | tf_op jit(solution)/shard_map/ppermute | solution.py:20
  112.6 36.0 %collective-permute-start.24 = (bf16[256,1024]{1,0:T(8,128)(2,1)S(1)}, bf16[256,1024]{1,0:T(8,128)(2,1)S(1)}, u32[]{:S(2)}, u32[]{:S(2)}) collective-permute-start(bf16[256,1024]{1,0:T(8,128)(2,1)S(1)} %get-tuple-element.158), channel_id=1, source_target_pairs={{0,1},{1,0},{2,3},{3,2},{4,5},{5,4},{6,7},{7,6},{8,9},{9,8},{10,11... | collective-permute-start | bytes 1572872 | tf_op jit(solution)/shard_map/ppermute | solution.py:25
  116.9 11.2 %collective-permute-start.20 = (bf16[384,512]{1,0:T(8,128)(2,1)S(1)}, bf16[384,512]{1,0:T(8,128)(2,1)S(1)}, u32[]{:S(2)}, u32[]{:S(2)}) collective-permute-start(bf16[384,512]{1,0:T(8,128)(2,1)S(1)} %get-tuple-element.154.refs_0_), channel_id=1, source_target_pairs={{0,8},{4,12},{8,0},{12,4},{16,24},{20,28},{24,16},{28,20},{1,9},{5... | collective-permute-start | bytes 1179656 | tf_op jit(solution)/shard_map/ppermute | solution.py:20
  118.4 10.9 %collective-permute-start.21 = (bf16[384,512]{1,0:T(8,128)(2,1)S(1)}, bf16[384,512]{1,0:T(8,128)(2,1)S(1)}, u32[]{:S(2)}, u32[]{:S(2)}) collective-permute-start(bf16[384,512]{1,0:T(8,128)(2,1)S(1)} %get-tuple-element.155.refs_2_), channel_id=1, source_target_pairs={{0,16},{4,20},{8,24},{12,28},{16,0},{20,4},{24,8},{28,12},{1,17},{... | collective-permute-start | bytes 1179656 | tf_op jit(solution)/shard_map/ppermute | solution.py:20
  130.7 18.6 %collective-permute-start.22 = (bf16[768,512]{1,0:T(8,128)(2,1)S(1)}, bf16[768,512]{1,0:T(8,128)(2,1)S(1)}, u32[]{:S(2)}, u32[]{:S(2)}) collective-permute-start(bf16[768,512]{1,0:T(8,128)(2,1)S(1)} %get-tuple-element.156.refs_0_), channel_id=1, source_target_pairs={{0,16},{4,20},{8,24},{12,28},{16,0},{20,4},{24,8},{28,12},{1,17},{... | collective-permute-start | bytes 2359304 | tf_op jit(solution)/shard_map/ppermute | solution.py:20
  131.2 18.2 %collective-permute-start.23 = (bf16[768,512]{1,0:T(8,128)(2,1)S(1)}, bf16[768,512]{1,0:T(8,128)(2,1)S(1)}, u32[]{:S(2)}, u32[]{:S(2)}) collective-permute-start(bf16[768,512]{1,0:T(8,128)(2,1)S(1)} %get-tuple-element.157.refs_2_), channel_id=1, source_target_pairs={{0,8},{4,12},{8,0},{12,4},{16,24},{20,28},{24,16},{28,20},{1,9},{5... | collective-permute-start | bytes 2359304 | tf_op jit(solution)/shard_map/ppermute | solution.py:20
  151.4 16.3 %collective-permute-start.25 = (bf16[3072,512]{1,0:T(8,128)(2,1)}, bf16[3072,512]{1,0:T(8,128)(2,1)}, u32[]{:S(2)}, u32[]{:S(2)}) collective-permute-start(bf16[3072,512]{1,0:T(8,128)(2,1)} %get-tuple-element.159.refs_2_.refs_0_), channel_id=1, source_target_pairs={{0,4},{4,0},{8,12},{12,8},{16,20},{20,16},{24,28},{28,24},{1,5},{5... | collective-permute-start | bytes 9437192 | tf_op jit(solution)/shard_map/ppermute | solution.py:20
  151.5 24.7 %all-to-all-start.1 = ((bf16[8,64,1024]{2,1,0:T(8,128)(2,1)}), bf16[8,64,1024]{2,1,0:T(8,128)(2,1)}, u32[]{:S(2)}, u32[]{:S(2)}) async-start(bf16[8,64,1024]{2,1,0:T(8,128)(2,1)} %bitcast.150), calls=%async_computation.1 | async-start | bytes 2097152 | tf_op jit(solution)/shard_map/all_to_all | solution.py:947
  161.1 18.2 %collective-permute-start.26 = (bf16[384,512]{1,0:T(8,128)(2,1)}, bf16[384,512]{1,0:T(8,128)(2,1)S(1)}, u32[]{:S(2)}, u32[]{:S(2)}) collective-permute-start(bf16[384,512]{1,0:T(8,128)(2,1)} %get-tuple-element.166.refs_0_), channel_id=1, source_target_pairs={{0,8},{4,12},{8,0},{12,4},{16,24},{20,28},{24,16},{28,20},{1,9},{5... | collective-permute-start | bytes 1179656 | tf_op jit(solution)/shard_map/ppermute | solution.py:20
  163.1 16.2 %collective-permute-start.27 = (bf16[384,512]{1,0:T(8,128)(2,1)}, bf16[384,512]{1,0:T(8,128)(2,1)}, u32[]{:S(2)}, u32[]{:S(2)}) collective-permute-start(bf16[384,512]{1,0:T(8,128)(2,1)} %get-tuple-element.167.refs_2_), channel_id=1, source_target_pairs={{0,16},{4,20},{8,24},{12,28},{16,0},{20,4},{24,8},{28,12},{1,17},{... | collective-permute-start | bytes 1179656 | tf_op jit(solution)/shard_map/ppermute | solution.py:20
  184.0 24.3 %collective-permute-start.28 = (bf16[768,512]{1,0:T(8,128)(2,1)S(1)}, bf16[768,512]{1,0:T(8,128)(2,1)S(1)}, u32[]{:S(2)}, u32[]{:S(2)}) collective-permute-start(bf16[768,512]{1,0:T(8,128)(2,1)S(1)} %get-tuple-element.170.refs_0_), channel_id=1, source_target_pairs={{0,16},{4,20},{8,24},{12,28},{16,0},{20,4},{24,8},{28,12},{1,17},{... | collective-permute-start | bytes 2359304 | tf_op jit(solution)/shard_map/ppermute | solution.py:20
  184.8 23.5 %collective-permute-start.29 = (bf16[768,512]{1,0:T(8,128)(2,1)S(1)}, bf16[768,512]{1,0:T(8,128)(2,1)S(1)}, u32[]{:S(2)}, u32[]{:S(2)}) collective-permute-start(bf16[768,512]{1,0:T(8,128)(2,1)S(1)} %get-tuple-element.171.refs_2_), channel_id=1, source_target_pairs={{0,8},{4,12},{8,0},{12,4},{16,24},{20,28},{24,16},{28,20},{1,9},{5... | collective-permute-start | bytes 2359304 | tf_op jit(solution)/shard_map/ppermute | solution.py:20
  186.0 12.3 %collective-permute-start.30 = (f32[1,1]{1,0:T(1,128)}, f32[1,1]{1,0:T(1,128)}, u32[]{:S(2)}, u32[]{:S(2)}) collective-permute-start(f32[1,1]{1,0:T(1,128)} %add.318), channel_id=1, source_target_pairs={{0,2},{1,3},{2,0},{3,1},{4,6},{5,7},{6,4},{7,5},{8,10},{9,11},{10,... | collective-permute-start | bytes 20 | tf_op jit(solution)/shard_map/ppermute | solution.py:25
  209.1 9.4 %collective-permute-start.32 = (bf16[3072,512]{1,0:T(8,128)(2,1)S(1)}, bf16[3072,512]{1,0:T(8,128)(2,1)S(1)}, u32[]{:S(2)}, u32[]{:S(2)}) collective-permute-start(bf16[3072,512]{1,0:T(8,128)(2,1)S(1)} %get-tuple-element.174.refs_0_), channel_id=1, source_target_pairs={{0,4},{4,0},{8,12},{12,8},{16,20},{20,16},{24,28},{28,24},{1,5},{5... | collective-permute-start | bytes 9437192 | tf_op jit(solution)/shard_map/ppermute | solution.py:20
  209.2 25.3 %collective-permute-start.33 = (bf16[4,512,1024]{2,1,0:T(8,128)(2,1)}, bf16[4,512,1024]{2,1,0:T(8,128)(2,1)S(1)}, u32[]{:S(2)}, u32[]{:S(2)}) collective-permute-start(bf16[4,512,1024]{2,1,0:T(8,128)(2,1)} %get-tuple-element.173.refs_4_), channel_id=1, source_target_pairs={{0,4},{4,0},{8,12},{12,8},{16,20},{20,16},{24,28},{28,24},{1,5},{5... | collective-permute-start | bytes 12582920 | tf_op jit(solution)/shard_map/ppermute | solution.py:20
  234.4 44.2 %collective-permute-start.38 = (bf16[4,128,4096]{2,1,0:T(8,128)(2,1)}, bf16[4,128,4096]{2,1,0:T(8,128)(2,1)}, u32[]{:S(2)}, u32[]{:S(2)}) collective-permute-start(bf16[4,128,4096]{2,1,0:T(8,128)(2,1)} %get-tuple-element.177.refs_3_), channel_id=1, source_target_pairs={{0,4},{4,0},{8,12},{12,8},{16,20},{20,16},{24,28},{28,24},{1,5},{5... | collective-permute-start | bytes 12582920 | tf_op jit(solution)/shard_map/ppermute | solution.py:20
  241.8 25.6 %collective-permute-start.34 = (bf16[2,512,512]{2,1,0:T(8,128)(2,1)}, bf16[2,512,512]{2,1,0:T(8,128)(2,1)S(1)}, u32[]{:S(2)}, u32[]{:S(2)}) collective-permute-start(bf16[2,512,512]{2,1,0:T(8,128)(2,1)} %get-tuple-element.179), channel_id=1, source_target_pairs={{0,8},{4,12},{8,0},{12,4},{16,24},{20,28},{24,16},{28,20},{1,9},{5... | collective-permute-start | bytes 3145736 | tf_op jit(solution)/shard_map/ppermute | solution.py:20
  243.3 25.3 %collective-permute-start.35 = (bf16[2,512,512]{2,1,0:T(8,128)(2,1)}, bf16[2,512,512]{2,1,0:T(8,128)(2,1)S(1)}, u32[]{:S(2)}, u32[]{:S(2)}) collective-permute-start(bf16[2,512,512]{2,1,0:T(8,128)(2,1)} %get-tuple-element.180), channel_id=1, source_target_pairs={{0,16},{4,20},{8,24},{12,28},{16,0},{20,4},{24,8},{28,12},{1,17},{... | collective-permute-start | bytes 3145736 | tf_op jit(solution)/shard_map/ppermute | solution.py:20
  258.1 20.5 %collective-permute-start.39 = (bf16[4,128,1024]{2,1,0:T(8,128)(2,1)}, bf16[4,128,1024]{2,1,0:T(8,128)(2,1)}, u32[]{:S(2)}, u32[]{:S(2)}) collective-permute-start(bf16[4,128,1024]{2,1,0:T(8,128)(2,1)} %get-tuple-element.187), channel_id=1, source_target_pairs={{0,4},{4,0},{8,12},{12,8},{16,20},{20,16},{24,28},{28,24},{1,5},{5... | collective-permute-start | bytes 3145736 | tf_op jit(solution)/shard_map/ppermute | solution.py:20
  269.7 26.1 %collective-permute-start.36 = (bf16[512,512]{1,0:T(8,128)(2,1)}, bf16[512,512]{1,0:T(8,128)(2,1)}, u32[]{:S(2)}, u32[]{:S(2)}) collective-permute-start(bf16[512,512]{1,0:T(8,128)(2,1)} %fusion.15), channel_id=1, source_target_pairs={{0,16},{4,20},{8,24},{12,28},{16,0},{20,4},{24,8},{28,12},{1,17},{... | collective-permute-start | bytes 1572872 | tf_op jit(solution)/shard_map/ppermute | solution.py:20
  271.9 23.9 %collective-permute-start.37 = (bf16[512,512]{1,0:T(8,128)(2,1)}, bf16[512,512]{1,0:T(8,128)(2,1)}, u32[]{:S(2)}, u32[]{:S(2)}) collective-permute-start(bf16[512,512]{1,0:T(8,128)(2,1)} %fusion.16), channel_id=1, source_target_pairs={{0,8},{4,12},{8,0},{12,4},{16,24},{20,28},{24,16},{28,20},{1,9},{5... | collective-permute-start | bytes 1572872 | tf_op jit(solution)/shard_map/ppermute | solution.py:20
  274.4 29.3 %all-to-all-start.2 = ((bf16[8,64,1024]{2,1,0:T(8,128)(2,1)}), bf16[8,64,1024]{2,1,0:T(8,128)(2,1)}, u32[]{:S(2)}, u32[]{:S(2)}) async-start(bf16[8,64,1024]{2,1,0:T(8,128)(2,1)} %bitcast.28), calls=%async_computation.2 | async-start | bytes 2097152 | tf_op jit(solution)/shard_map/all_to_all | solution.py:947
  292.4 45.9 %collective-permute-start.40 = (bf16[2,128,2560]{2,1,0:T(8,128)(2,1)}, bf16[2,128,2560]{2,1,0:T(8,128)(2,1)}, u32[]{:S(2)}, u32[]{:S(2)}) collective-permute-start(bf16[2,128,2560]{2,1,0:T(8,128)(2,1)} %get-tuple-element.192), channel_id=1, source_target_pairs={{0,8},{4,12},{8,0},{12,4},{16,24},{20,28},{24,16},{28,20},{1,9},{5... | collective-permute-start | bytes 3932168 | tf_op jit(solution)/shard_map/ppermute | solution.py:20
  294.3 44.0 %collective-permute-start.41 = (bf16[2,128,2560]{2,1,0:T(8,128)(2,1)}, bf16[2,128,2560]{2,1,0:T(8,128)(2,1)}, u32[]{:S(2)}, u32[]{:S(2)}) collective-permute-start(bf16[2,128,2560]{2,1,0:T(8,128)(2,1)} %get-tuple-element.193), channel_id=1, source_target_pairs={{0,16},{4,20},{8,24},{12,28},{16,0},{20,4},{24,8},{28,12},{1,17},{... | collective-permute-start | bytes 3932168 | tf_op jit(solution)/shard_map/ppermute | solution.py:20
  299.6 38.7 %collective-permute-start.42 = (bf16[512,1024]{1,0:T(8,128)(2,1)}, bf16[512,1024]{1,0:T(8,128)(2,1)}, u32[]{:S(2)}, u32[]{:S(2)}) collective-permute-start(bf16[512,1024]{1,0:T(8,128)(2,1)} %pad_maximum_fusion.2.refs_0_), channel_id=1, source_target_pairs={{0,1},{3,2},{4,5},{7,6},{8,9},{11,10},{12,13},{15,14},{16,17},{19,... | collective-permute-start | bytes 3145736 | tf_op jit(solution)/shard_map/ppermute | solution.py:669
  333.7 19.8 %all-to-all-start.3 = ((bf16[8,64,1024]{2,1,0:T(8,128)(2,1)}), bf16[8,64,1024]{2,1,0:T(8,128)(2,1)}, u32[]{:S(2)}, u32[]{:S(2)}) async-start(bf16[8,64,1024]{2,1,0:T(8,128)(2,1)} %bitcast.31), calls=%async_computation.3 | async-start | bytes 2097152 | tf_op jit(solution)/shard_map/all_to_all | solution.py:947
  340.9 46.7 %collective-permute-start.43 = (bf16[512,1024]{1,0:T(8,128)(2,1)}, bf16[512,1024]{1,0:T(8,128)(2,1)}, u32[]{:S(2)}, u32[]{:S(2)}) collective-permute-start(bf16[512,1024]{1,0:T(8,128)(2,1)} %add_convert_fusion.4), channel_id=1, source_target_pairs={{1,2},{2,1},{5,6},{6,5},{9,10},{10,9},{13,14},{14,13},{17,18},{18,... | collective-permute-start | bytes 3145736 | tf_op jit(solution)/shard_map/ppermute | solution.py:669
  358.3 13.6 %collective-permute-start.45 = (bf16[128,2560]{1,0:T(8,128)(2,1)S(1)}, bf16[128,2560]{1,0:T(8,128)(2,1)S(1)}, u32[]{:S(2)}, u32[]{:S(2)}) collective-permute-start(bf16[128,2560]{1,0:T(8,128)(2,1)S(1)} %fusion.13), channel_id=1, source_target_pairs={{0,16},{4,20},{8,24},{12,28},{16,0},{20,4},{24,8},{28,12},{1,17},{... | collective-permute-start | bytes 1966088 | tf_op jit(solution)/shard_map/ppermute | solution.py:20
  360.1 15.1 %collective-permute-start.46 = (bf16[128,2560]{1,0:T(8,128)(2,1)S(1)}, bf16[128,2560]{1,0:T(8,128)(2,1)S(1)}, u32[]{:S(2)}, u32[]{:S(2)}) collective-permute-start(bf16[128,2560]{1,0:T(8,128)(2,1)S(1)} %fusion.14), channel_id=1, source_target_pairs={{0,8},{4,12},{8,0},{12,4},{16,24},{20,28},{24,16},{28,20},{1,9},{5... | collective-permute-start | bytes 1966088 | tf_op jit(solution)/shard_map/ppermute | solution.py:20
  362.7 18.6 %collective-permute-start.49 = (bf16[4,128,3072]{2,1,0:T(8,128)(2,1)S(1)}, bf16[4,128,3072]{2,1,0:T(8,128)(2,1)S(1)}, u32[]{:S(2)}, u32[]{:S(2)}) collective-permute-start(bf16[4,128,3072]{2,1,0:T(8,128)(2,1)S(1)} %copy-done.81), channel_id=1, source_target_pairs={{0,4},{4,0},{8,12},{12,8},{16,20},{20,16},{24,28},{28,24},{1,5},{5... | collective-permute-start | bytes 9437192 | tf_op jit(solution)/shard_map/ppermute | solution.py:20
  368.4 17.0 %collective-permute-start.44 = (bf16[4,256,1024]{2,1,0:T(8,128)(2,1)S(1)}, bf16[4,256,1024]{2,1,0:T(8,128)(2,1)S(1)}, u32[]{:S(2)}, u32[]{:S(2)}) collective-permute-start(bf16[4,256,1024]{2,1,0:T(8,128)(2,1)S(1)} %get-tuple-element.204), channel_id=1, source_target_pairs={{0,4},{4,0},{8,12},{12,8},{16,20},{20,16},{24,28},{28,24},{1,5},{5... | collective-permute-start | bytes 6291464 | tf_op jit(solution)/shard_map/ppermute | solution.py:20
  379.9 28.0 %collective-permute-start.52 = (bf16[128,5120]{1,0:T(8,128)(2,1)S(1)}, bf16[128,5120]{1,0:T(8,128)(2,1)S(1)}, u32[]{:S(2)}, u32[]{:S(2)}) collective-permute-start(bf16[128,5120]{1,0:T(8,128)(2,1)S(1)} %pad_maximum_fusion.1), channel_id=1, source_target_pairs={{0,1},{3,2},{4,5},{7,6},{8,9},{11,10},{12,13},{15,14},{16,17},{19,... | collective-permute-start | bytes 3932168 | tf_op jit(solution)/shard_map/ppermute | solution.py:669
  388.1 21.8 %collective-permute-start.50 = (bf16[2,128,1536]{2,1,0:T(8,128)(2,1)S(1)}, bf16[2,128,1536]{2,1,0:T(8,128)(2,1)S(1)}, u32[]{:S(2)}, u32[]{:S(2)}) collective-permute-start(bf16[2,128,1536]{2,1,0:T(8,128)(2,1)S(1)} %get-tuple-element.219), channel_id=1, source_target_pairs={{0,8},{4,12},{8,0},{12,4},{16,24},{20,28},{24,16},{28,20},{1,9},{5... | collective-permute-start | bytes 2359304 | tf_op jit(solution)/shard_map/ppermute | solution.py:20
  388.4 21.5 %collective-permute-start.51 = (bf16[2,128,1536]{2,1,0:T(8,128)(2,1)S(1)}, bf16[2,128,1536]{2,1,0:T(8,128)(2,1)S(1)}, u32[]{:S(2)}, u32[]{:S(2)}) collective-permute-start(bf16[2,128,1536]{2,1,0:T(8,128)(2,1)S(1)} %get-tuple-element.220), channel_id=1, source_target_pairs={{0,16},{4,20},{8,24},{12,28},{16,0},{20,4},{24,8},{28,12},{1,17},{... | collective-permute-start | bytes 2359304 | tf_op jit(solution)/shard_map/ppermute | solution.py:20
  392.2 30.6 %collective-permute-start.55 = (bf16[512,1024]{1,0:T(8,128)(2,1)S(1)}, bf16[512,1024]{1,0:T(8,128)(2,1)S(1)}, u32[]{:S(2)}, u32[]{:S(2)}) collective-permute-start(bf16[512,1024]{1,0:T(8,128)(2,1)S(1)} %add_convert_fusion.3), channel_id=1, source_target_pairs={{1,0},{2,3},{5,4},{6,7},{9,8},{10,11},{13,12},{14,15},{17,16},{18,... | collective-permute-start | bytes 3145736 | tf_op jit(solution)/shard_map/ppermute | solution.py:669
  393.5 26.3 %collective-permute-start.56 = (bf16[2,256,512]{2,1,0:T(8,128)(2,1)S(1)}, bf16[2,256,512]{2,1,0:T(8,128)(2,1)S(1)}, u32[]{:S(2)}, u32[]{:S(2)}) collective-permute-start(bf16[2,256,512]{2,1,0:T(8,128)(2,1)S(1)} %get-tuple-element.231), channel_id=1, source_target_pairs={{0,8},{4,12},{8,0},{12,4},{16,24},{20,28},{24,16},{28,20},{1,9},{5... | collective-permute-start | bytes 1572872 | tf_op jit(solution)/shard_map/ppermute | solution.py:20
  407.9 14.9 %collective-permute-start.57 = (bf16[2,256,512]{2,1,0:T(8,128)(2,1)S(1)}, bf16[2,256,512]{2,1,0:T(8,128)(2,1)S(1)}, u32[]{:S(2)}, u32[]{:S(2)}) collective-permute-start(bf16[2,256,512]{2,1,0:T(8,128)(2,1)S(1)} %get-tuple-element.232), channel_id=1, source_target_pairs={{0,16},{4,20},{8,24},{12,28},{16,0},{20,4},{24,8},{28,12},{1,17},{... | collective-permute-start | bytes 1572872 | tf_op jit(solution)/shard_map/ppermute | solution.py:20
  410.1 18.4 %collective-permute-start.53 = (bf16[128,1536]{1,0:T(8,128)(2,1)S(1)}, bf16[128,1536]{1,0:T(8,128)(2,1)S(1)}, u32[]{:S(2)}, u32[]{:S(2)}) collective-permute-start(bf16[128,1536]{1,0:T(8,128)(2,1)S(1)} %fusion.20), channel_id=1, source_target_pairs={{0,16},{4,20},{8,24},{12,28},{16,0},{20,4},{24,8},{28,12},{1,17},{... | collective-permute-start | bytes 1179656 | tf_op jit(solution)/shard_map/ppermute | solution.py:20
  410.6 17.9 %collective-permute-start.54 = (bf16[128,1536]{1,0:T(8,128)(2,1)S(1)}, bf16[128,1536]{1,0:T(8,128)(2,1)S(1)}, u32[]{:S(2)}, u32[]{:S(2)}) collective-permute-start(bf16[128,1536]{1,0:T(8,128)(2,1)S(1)} %fusion.21), channel_id=1, source_target_pairs={{0,8},{4,12},{8,0},{12,4},{16,24},{20,28},{24,16},{28,20},{1,9},{5... | collective-permute-start | bytes 1179656 | tf_op jit(solution)/shard_map/ppermute | solution.py:20
  419.9 20.0 %collective-permute-start.59 = (bf16[128,5120]{1,0:T(8,128)(2,1)S(1)}, bf16[128,5120]{1,0:T(8,128)(2,1)S(1)}, u32[]{:S(2)}, u32[]{:S(2)}) collective-permute-start(bf16[128,5120]{1,0:T(8,128)(2,1)S(1)} %add_convert_fusion.2), channel_id=1, source_target_pairs={{1,2},{2,1},{5,6},{6,5},{9,10},{10,9},{13,14},{14,13},{17,18},{18,... | collective-permute-start | bytes 3932168 | tf_op jit(solution)/shard_map/ppermute | solution.py:669
  428.9 10.9 %collective-permute-start.58 = (bf16[64,3072]{1,0:T(8,128)(2,1)S(1)}, bf16[64,3072]{1,0:T(8,128)(2,1)S(1)}, u32[]{:S(2)}, u32[]{:S(2)}) collective-permute-start(bf16[64,3072]{1,0:T(8,128)(2,1)S(1)} %fusion.23), channel_id=1, source_target_pairs={{0,1},{1,0},{2,3},{3,2},{4,5},{5,4},{6,7},{7,6},{8,9},{9,8},{10,11... | collective-permute-start | bytes 1179656 | tf_op jit(solution)/shard_map/ppermute | solution.py:25
  445.2 17.3 %collective-permute-start.64 = (bf16[160,1024]{1,0:T(8,128)(2,1)S(1)}, bf16[160,1024]{1,0:T(8,128)(2,1)S(1)}, u32[]{:S(2)}, u32[]{:S(2)}) collective-permute-start(bf16[160,1024]{1,0:T(8,128)(2,1)S(1)} %constant_dynamic-slice_fusion.1), channel_id=1, source_target_pairs={{0,1},{1,0},{2,3},{3,2},{4,5},{5,4},{6,7},{7,6},{8,9},{9,8},{10,11... | collective-permute-start | bytes 983048 | tf_op jit(solution)/shard_map/ppermute | solution.py:25
  451.6 34.1 %collective-permute-start.65 = (bf16[128,5120]{1,0:T(8,128)(2,1)S(1)}, bf16[128,5120]{1,0:T(8,128)(2,1)S(1)}, u32[]{:S(2)}, u32[]{:S(2)}) collective-permute-start(bf16[128,5120]{1,0:T(8,128)(2,1)S(1)} %add_convert_fusion.1), channel_id=1, source_target_pairs={{1,0},{2,3},{5,4},{6,7},{9,8},{10,11},{13,12},{14,15},{17,16},{18,... | collective-permute-start | bytes 3932168 | tf_op jit(solution)/shard_map/ppermute | solution.py:669
  453.0 9.1 %collective-permute-start.63 = (bf16[32,3072]{1,0:T(8,128)(2,1)S(1)}, bf16[32,3072]{1,0:T(8,128)(2,1)S(1)}, u32[]{:S(2)}, u32[]{:S(2)}) collective-permute-start(bf16[32,3072]{1,0:T(8,128)(2,1)S(1)} %constant_dynamic-slice_fusion.2), channel_id=1, source_target_pairs={{0,2},{1,3},{2,0},{3,1},{4,6},{5,7},{6,4},{7,5},{8,10},{9,11},{10,... | collective-permute-start | bytes 589832 | tf_op jit(solution)/shard_map/ppermute | solution.py:25
  485.7 13.7 %collective-permute-start.66 = (bf16[32,3072]{1,0:T(8,128)(2,1)S(1)}, bf16[32,3072]{1,0:T(8,128)(2,1)S(1)}, u32[]{:S(2)}, u32[]{:S(2)}) collective-permute-start(bf16[32,3072]{1,0:T(8,128)(2,1)S(1)} %add_convert_fusion.18), channel_id=1, source_target_pairs={{0,2},{1,3},{2,0},{3,1},{4,6},{5,7},{6,4},{7,5},{8,10},{9,11},{10,... | collective-permute-start | bytes 589832 | tf_op jit(solution)/shard_map/ppermute | solution.py:25
  486.0 13.4 %collective-permute-start.67 = (bf16[80,1024]{1,0:T(8,128)(2,1)S(1)}, bf16[80,1024]{1,0:T(8,128)(2,1)S(1)}, u32[]{:S(2)}, u32[]{:S(2)}) collective-permute-start(bf16[80,1024]{1,0:T(8,128)(2,1)S(1)} %constant_dynamic-slice_fusion), channel_id=1, source_target_pairs={{0,2},{1,3},{2,0},{3,1},{4,6},{5,7},{6,4},{7,5},{8,10},{9,11},{10,... | collective-permute-start | bytes 491528 | tf_op jit(solution)/shard_map/ppermute | solution.py:25
  499.4 13.0 %collective-permute-start.68 = (bf16[64,3072]{1,0:T(8,128)(2,1)S(1)}, bf16[64,3072]{1,0:T(8,128)(2,1)S(1)}, u32[]{:S(2)}, u32[]{:S(2)}) collective-permute-start(bf16[64,3072]{1,0:T(8,128)(2,1)S(1)} %pad_maximum_fusion.4), channel_id=1, source_target_pairs={{0,1},{1,0},{2,3},{3,2},{4,5},{5,4},{6,7},{7,6},{8,9},{9,8},{10,11... | collective-permute-start | bytes 1179656 | tf_op jit(solution)/shard_map/ppermute | solution.py:25
  499.6 10.7 %collective-permute-start.69 = (bf16[80,1024]{1,0:T(8,128)(2,1)S(1)}, bf16[80,1024]{1,0:T(8,128)(2,1)S(1)}, u32[]{:S(2)}, u32[]{:S(2)}) collective-permute-start(bf16[80,1024]{1,0:T(8,128)(2,1)S(1)} %add_convert_fusion.19), channel_id=1, source_target_pairs={{0,2},{1,3},{2,0},{3,1},{4,6},{5,7},{6,4},{7,5},{8,10},{9,11},{10,... | collective-permute-start | bytes 491528 | tf_op jit(solution)/shard_map/ppermute | solution.py:25
  512.5 8.6 %collective-permute-start.70 = (bf16[160,1024]{1,0:T(8,128)(2,1)S(1)}, bf16[160,1024]{1,0:T(8,128)(2,1)S(1)}, u32[]{:S(2)}, u32[]{:S(2)}) collective-permute-start(bf16[160,1024]{1,0:T(8,128)(2,1)S(1)} %pad_maximum_fusion.5), channel_id=1, source_target_pairs={{0,1},{1,0},{2,3},{3,2},{4,5},{5,4},{6,7},{7,6},{8,9},{9,8},{10,11... | collective-permute-start | bytes 983048 | tf_op jit(solution)/shard_map/ppermute | solution.py:25
  (145 other events, 1040.4 us)
